TPU v7x, 512 devices: a whole 4x8x8 slice. The times are simulated.
512 devices in a mesh: tm: 2 (over core), space: 256 (over z, y, x).
Axes of the slice: x: 4, y: 8, z: 8, core: 2. Of those that a mesh axis runs over, the one named last changes fastest.
Arguments:
- adj_source: float32 [32, 2, 131072], P('tm', None, 'space'), may hold values from -4 to 6
- terminal: float32 [2, 131072], P(None, 'space'), may hold values from -4 to 6
- capacity: float32 [131072], P('space'), may hold values from 0.2 to 2
- blocks: float32 [2048, 7, 64, 64], P('space'), as said below
- columns: int32 [2048, 7], P('space'), may hold values from 0 to 15, as said below
- face_lists: int32 [256, 2, 4], P('space'), may hold values from 0 to 7, as said below
Outputs:
- adjoint: float32 [32, 2, 131072], P('tm', None, 'space')
Inputs may be any that keep to these rules, and one draw needn't show every extreme that they name: `columns`: entry 0 of each block row is the row's own block (local id R mod 8); entry 1 is one of the 8 received blocks; ids may repeat within a row. `face_lists`: each list holds 4 distinct own blocks; the two lists of a shard are disjoint; block 0 is always sent to the lower shard and block 7 to the upper one. `blocks`: in every row of a block row, the diagonal entry of the own block exceeds the sum of magnitudes of all other entries of that row.
All inputs are finite; a program needn't handle non-finite values.
Results may differ from a plain program's by a relative error of at most 0.0001.
Values sent between devices are 32-bit elements; how exact they have to be, the bound alone decides.
A program may use at most 64 MiB of HBM per device.

v0:
```python
import functools
import math

import jax
import jax.numpy as jnp
import numpy as np
from jax import lax
from jax.experimental import pallas as pl
from jax.experimental.pallas import tpu as pltpu
from jax.sharding import PartitionSpec as P

OUTER = 3
SWEEPS = 3
STEPS = 32
HALF = STEPS // 2
CORNER_WEIGHT = 0.1
ROOT = CORNER_WEIGHT ** (1.0 / STEPS)
ROUNDS = OUTER * SWEEPS - 1
BLOCK = 64
LANES = 128
MESH = pl.DeviceIdType.MESH


def split(value):
    high = value.astype(jnp.bfloat16)
    low = (value - high.astype(jnp.float32)).astype(jnp.bfloat16)
    return high, low


def split_table(table):
    high = table.astype(jnp.bfloat16)
    low = (table - high.astype(np.float64)).astype(jnp.bfloat16)
    return np.concatenate([high, high, low], axis=1)


def tables():
    steps = np.arange(STEPS)
    modes = np.arange(HALF)
    angles = 2.0 * np.pi * ((modes[:, None] * steps[None, :]) % STEPS) / STEPS
    nyquist = (-1.0) ** steps
    cosines, sines = np.cos(angles), -np.sin(angles)
    sines[0] = nyquist
    basis = np.concatenate([cosines, sines], axis=0)
    scale = CORNER_WEIGHT ** (steps / STEPS)
    forward = basis * scale[None, :]
    weight = np.full((STEPS,), 2.0)
    weight[0] = weight[HALF] = 1.0
    inverse = (basis * weight[:, None]).T / STEPS
    last = inverse[STEPS - 1] * ROOT
    backward = inverse / scale[:, None]
    real_coef = 1.0 - ROOT * np.cos(2.0 * np.pi * modes / STEPS)
    imag_coef = ROOT * np.sin(2.0 * np.pi * modes / STEPS)
    real_low = real_coef.copy()
    real_low[0] = 1.0 + ROOT
    columns = np.zeros((STEPS, LANES), np.float32)
    columns[:HALF, 0] = real_coef
    columns[HALF:, 0] = real_low
    columns[:HALF, 1] = imag_coef
    columns[:, 2] = last
    return split_table(forward), split_table(backward), columns


def product(table, value):
    high, low = split(value)
    return jnp.dot(
        table, jnp.concatenate([high, low, high], axis=0), preferred_element_type=jnp.float32
    )


def reorder(value, ids):
    lower_half = lax.broadcasted_iota(jnp.int32, (1, LANES), 1) < BLOCK
    both = []
    for tile in range(4):
        plain = value[:, tile * LANES : (tile + 1) * LANES]
        turned = pltpu.roll(plain, BLOCK, 1)
        both.append(jnp.where(lower_half, plain, turned))
        both.append(jnp.where(lower_half, turned, plain))
    tiles = []
    for tile in range(4):
        wanted = jnp.where(lower_half, ids[2 * tile], ids[2 * tile + 1])
        total = both[0]
        for block in range(1, 8):
            total = jnp.where(wanted == block, both[block], total)
        tiles.append(total)
    return jnp.concatenate(tiles, axis=1)


def kernel(
    adj, term, cap, cols, faces, forward, backward, coefs, blocks_hbm, out,
    blk, turned, mat_high, mat_low, diag, recip, capacity, xsend, xrecv, wsend, wrecv,
    total, ysend, yrecv, blk_sem, tm_sems, send_sems, recv_sems,
):
    group = lax.axis_index("tm")
    shard = lax.axis_index("space")
    shards = lax.axis_size("space")
    other = 1 - group
    lower = lax.rem(shard + shards - 1, shards)
    upper = lax.rem(shard + 1, shards)
    first = group == 0

    blk_copy = pltpu.make_async_copy(blocks_hbm, blk, blk_sem)
    blk_copy.start()

    barrier = pltpu.get_barrier_semaphore()
    for target in ((other, shard), (group, lower), (group, upper)):
        pl.semaphore_signal(barrier, inc=1, device_id=target, device_id_type=MESH)
    case_0 = adj[:, 0, :]
    case_1 = adj[:, 1, :]
    xsend[...] = jnp.where(first, case_1, case_0)
    mine = jnp.where(first, case_0, case_1)
    pl.semaphore_wait(barrier, 3)

    xcopy = pltpu.make_async_remote_copy(
        src_ref=xsend, dst_ref=xrecv, send_sem=tm_sems.at[0], recv_sem=tm_sems.at[1],
        device_id=(other, shard), device_id_type=MESH,
    )
    xcopy.start()

    ids = [faces[i // 4, i % 4] for i in range(8)]
    cap_row = cap[...]
    capacity[...] = reorder(jnp.broadcast_to(cap_row, (8, 8 * BLOCK)), ids)
    blk_copy.wait()
    eye = lax.broadcasted_iota(jnp.int32, (BLOCK, BLOCK), 0) == lax.broadcasted_iota(
        jnp.int32, (BLOCK, BLOCK), 1
    )
    rows = [
        jnp.sum(jnp.where(eye, blk[ids[i], 0], 0.0), axis=0, keepdims=True) for i in range(8)
    ]
    diag[...] = jnp.broadcast_to(jnp.concatenate(rows, axis=1), diag.shape)
    cap_own = capacity[0:1, :]
    diag_own = diag[0:1, :]
    imag = coefs[0:HALF, 1:2] * cap_own
    for part in range(2):
        real = coefs[part * HALF : (part + 1) * HALF, 0:1] * cap_own + diag_own
        over = 1.0 / (real * real + imag * imag)
        recip[part] = real * over
        if part == 0:
            recip[2] = -imag * over

    def divided(value):
        upper_part, lower_part = value[:HALF], value[HALF:]
        return jnp.concatenate(
            [
                recip[0] * upper_part - recip[2] * lower_part,
                recip[2] * upper_part + recip[1] * lower_part,
            ],
            axis=0,
        )

    def halo(slot):
        down = pltpu.make_async_remote_copy(
            src_ref=wsend.at[slot, 0], dst_ref=wrecv.at[slot, 1],
            send_sem=send_sems.at[slot, 0], recv_sem=recv_sems.at[slot, 1],
            device_id=(group, lower), device_id_type=MESH,
        )
        up = pltpu.make_async_remote_copy(
            src_ref=wsend.at[slot, 1], dst_ref=wrecv.at[slot, 0],
            send_sem=send_sems.at[slot, 1], recv_sem=recv_sems.at[slot, 0],
            device_id=(group, upper), device_id_type=MESH,
        )
        return down, up

    def send(slot, value):
        wsend[slot, 0] = value[:, : 4 * BLOCK]
        wsend[slot, 1] = value[:, 4 * BLOCK :]
        down, up = halo(slot)
        down.start()
        up.start()

    xcopy.wait()
    theirs = xrecv[...]
    source = jnp.concatenate(
        [jnp.where(first, mine, theirs), jnp.where(first, theirs, mine)], axis=0
    )
    head = jnp.where(first, term[0:1, :], term[1:2, :]) * cap_row
    row_ids = lax.broadcasted_iota(jnp.int32, (STEPS, 1), 0)
    source = source + jnp.where(row_ids == 0, head, 0.0)
    spectrum = reorder(product(forward[...], source), ids)
    field = divided(spectrum)
    send(0, field)
    total[...] = jnp.zeros_like(total)

    lower_half = lax.broadcasted_iota(jnp.int32, (1, LANES), 1) < BLOCK
    turned_eye = lax.broadcasted_iota(jnp.int32, (BLOCK, LANES), 0) == lax.rem(
        lax.broadcasted_iota(jnp.int32, (BLOCK, LANES), 1), BLOCK
    )
    no_lower = shard == 0
    no_upper = shard == shards - 1
    for pair in range(4):
        left, right = ids[2 * pair], ids[2 * pair + 1]
        wanted = []
        for k in range(7):
            entry = jnp.concatenate([blk[left, k], blk[right, k]], axis=0)
            entry = -entry.T
            if k == 0:
                entry = jnp.where(turned_eye, 0.0, entry)
            turned[k] = entry
            wanted.append(jnp.where(lower_half, cols[left, k], cols[right, k]))
        for place in range(16):
            if place < 8:
                name = ids[place]
            elif place < 12:
                name = jnp.where(no_lower, -1, place)
            else:
                name = jnp.where(no_upper, -1, place)
            tile = jnp.where(wanted[0] == name, turned[0], 0.0)
            for k in range(1, 7):
                tile = tile + jnp.where(wanted[k] == name, turned[k], 0.0)
            high, low = split(tile)
            where = (slice(place * BLOCK, (place + 1) * BLOCK), slice(pair * LANES, (pair + 1) * LANES))
            mat_high[where] = high
            mat_low[where] = low

    def conduct(value, start, count):
        high, low = split(value)
        both = jnp.dot(
            jnp.concatenate([high, low], axis=0), mat_high[start : start + count, :],
            preferred_element_type=jnp.float32,
        )
        rest = jnp.dot(
            high, mat_low[start : start + count, :], preferred_element_type=jnp.float32
        )
        return both[:STEPS] + both[STEPS:] + rest

    real_rows = row_ids <= HALF
    last = coefs[:, 2:3]

    def round_of(slot, tail):
        value = jnp.concatenate([wsend[slot, 0], wsend[slot, 1]], axis=1)
        total[...] += value
        tail = tail + jnp.sum(value * last, axis=0, keepdims=True)
        closes = lax.rem(slot, SWEEPS) == SWEEPS - 1
        fix = jnp.where(closes, tail, 0.0) * capacity[0:1, :]
        tail = jnp.where(closes, 0.0, tail)
        result = conduct(value, 0, 8 * BLOCK) - jnp.where(real_rows, fix, 0.0)
        down, up = halo(slot)
        up.wait_recv()
        result = result + conduct(wrecv[slot, 0], 8 * BLOCK, 4 * BLOCK)
        down.wait_recv()
        result = result + conduct(wrecv[slot, 1], 12 * BLOCK, 4 * BLOCK)
        down.wait_send()
        up.wait_send()
        return divided(result), tail

    def step(slot, tail):
        value, tail = round_of(slot, tail)
        send(slot + 1, value)
        return tail

    tail = lax.fori_loop(0, ROUNDS - 1, step, jnp.zeros((1, 8 * BLOCK), jnp.float32))
    value, _ = round_of(ROUNDS - 1, tail)

    places = []
    for block in range(8):
        place = jnp.int32(0)
        for i in range(1, 8):
            place = place + jnp.where(ids[i] == block, i, 0)
        places.append(place)
    summed = product(backward[...], reorder(total[...] + value, places))
    early, late = summed[:HALF], summed[HALF:]
    ysend[...] = jnp.where(first, late, early)
    ycopy = pltpu.make_async_remote_copy(
        src_ref=ysend, dst_ref=yrecv, send_sem=tm_sems.at[2], recv_sem=tm_sems.at[3],
        device_id=(other, shard), device_id_type=MESH,
    )
    ycopy.start()
    kept = jnp.where(first, early, late)
    ycopy.wait()
    came = yrecv[...]
    out[:, 0, :] = jnp.where(first, kept, came)
    out[:, 1, :] = jnp.where(first, came, kept)


def per_device(adj_source, terminal, capacity, blocks, columns, face_lists):
    nodes = capacity.shape[0]
    forward, backward, coefs = tables()
    vmem = pl.BlockSpec(memory_space=pltpu.VMEM)
    smem = pl.BlockSpec(memory_space=pltpu.SMEM)
    f32, bf16 = jnp.float32, jnp.bfloat16
    return pl.pallas_call(
        kernel,
        out_shape=jax.ShapeDtypeStruct(adj_source.shape, f32),
        in_specs=[vmem, vmem, vmem, smem, smem, vmem, vmem, vmem, pl.BlockSpec(memory_space=pl.ANY)],
        out_specs=vmem,
        scratch_shapes=[
            pltpu.VMEM(blocks.shape, f32),
            pltpu.VMEM((7, BLOCK, LANES), f32),
            pltpu.VMEM((16 * BLOCK, nodes), bf16),
            pltpu.VMEM((16 * BLOCK, nodes), bf16),
            pltpu.VMEM((8, nodes), f32),
            pltpu.VMEM((3, HALF, nodes), f32),
            pltpu.VMEM((8, nodes), f32),
            pltpu.VMEM((HALF, nodes), f32),
            pltpu.VMEM((HALF, nodes), f32),
            pltpu.VMEM((ROUNDS, 2, STEPS, nodes // 2), f32),
            pltpu.VMEM((ROUNDS, 2, STEPS, nodes // 2), f32),
            pltpu.VMEM((STEPS, nodes), f32),
            pltpu.VMEM((HALF, nodes), f32),
            pltpu.VMEM((HALF, nodes), f32),
            pltpu.SemaphoreType.DMA,
            pltpu.SemaphoreType.DMA((4,)),
            pltpu.SemaphoreType.DMA((ROUNDS, 2)),
            pltpu.SemaphoreType.DMA((ROUNDS, 2)),
        ],
        compiler_params=pltpu.CompilerParams(
            collective_id=0, has_side_effects=True, vmem_limit_bytes=24 * 1024 * 1024
        ),
        name="window",
    )(
        adj_source, terminal, capacity.reshape(1, nodes), columns, face_lists.reshape(2, 4),
        jnp.asarray(forward), jnp.asarray(backward), jnp.asarray(coefs), blocks,
    )


def solution(mesh):
    return jax.shard_map(
        per_device,
        mesh=mesh,
        in_specs=(
            P("tm", None, "space"),
            P(None, "space"),
            P("space"),
            P("space", None, None, None),
            P("space", None),
            P("space", None, None),
        ),
        out_specs=P("tm", None, "space"),
        check_vma=False,
    )
```

profile of v0, /device:TPU:1, one launch (start us, length us, event | category | flops | bytes accessed | tf_op | source)
XLA Modules:
  0.0 74.7 jit_solution(15169093072894039887)
XLA Ops:
  0.0 0.0 copy-start
  0.0 1.5 %copy-done = f32[8,7,64,64]{3,2,1,0:T(8,128)S(1)} copy-done((f32[8,7,64,64]{3,2,1,0:T(8,128)S(1)}, f32[8,7,64,64]{3,2,1,0:T(8,128)}, u32[]{:S(2)}) %copy-start) | copy-done | bytes 917528
  1.5 0.0 copy-start.1
  1.5 0.8 %copy-done.1 = f32[16,2,512]{2,1,0:T(2,128)S(1)} copy-done((f32[16,2,512]{2,1,0:T(2,128)S(1)}, f32[16,2,512]{2,1,0:T(2,128)}, u32[]{:S(2)}) %copy-start.1) | copy-done | bytes 65560
  2.3 0.0 copy-start.2
  2.3 0.7 copy-done.2
  3.1 0.0 copy-start.3
  3.1 0.7 copy-done.3
  3.8 0.0 copy-start.4
  3.8 0.7 copy-done.4
  4.5 0.0 copy-start.5
  4.5 0.7 copy-done.5
  5.1 0.0 copy-start.6
  5.1 0.7 copy-done.6
  5.8 0.0 copy-start.7
  5.8 0.7 copy-done.7
  6.5 0.0 copy-start.8
  6.5 0.7 copy-done.8
  7.2 66.9 %window.1 = f32[16,2,512]{2,1,0:T(2,128)S(1)} custom-call(f32[16,2,512]{2,1,0:T(2,128)S(1)} %copy-done.1, f32[2,512]{1,0:T(2,128)S(1)} %copy-done.5, f32[1,512]{1,0:T(1,128)S(1)} %bitcast.2, s32[8,7]{1,0:T(8,128)S(1)} %copy-done.6, s32[2,4]{1,0:T(2,128)S(1)} %bitcast.3, bf16[32,96]{1,0:T(8,128)(2,1)S(1)} %copy-done.4, bf16[32,96]{1,0:T(8,128)(2,1)S(1)} %copy-done.3, ...), custom_call_target="tpu_custom_call" | custom-call | tf_op jit(solution)/shard_map/window/pallas_call | solution.py:280
  74.1 0.6 copy.11
Async XLA Ops:
  0.0 1.5 %copy-start = (f32[8,7,64,64]{3,2,1,0:T(8,128)S(1)}, f32[8,7,64,64]{3,2,1,0:T(8,128)}, u32[]{:S(2)}) copy-start(f32[8,7,64,64]{3,2,1,0:T(8,128)} %blocks_hbm.1) | copy-start | bytes 2752516
  1.5 0.8 %copy-start.1 = (f32[16,2,512]{2,1,0:T(2,128)S(1)}, f32[16,2,512]{2,1,0:T(2,128)}, u32[]{:S(2)}) copy-start(f32[16,2,512]{2,1,0:T(2,128)} %adj.1) | copy-start | bytes 196612
  2.3 0.7 copy-start.2
  3.1 0.7 copy-start.3
  3.8 0.7 copy-start.4
  4.5 0.7 copy-start.5
  5.1 0.7 copy-start.6
  5.8 0.7 copy-start.7
  6.5 0.7 copy-start.8
where the time goes:
time: 75.2 us; the launch traced here: 74.7 us
  Pallas kernels  66.9 us (89%)
  local copies, waits for them, and re-layouts  7.81 us (10%)
    pallas_call x1, Pallas kernels, per_device(): pl.pallas_call(kernel, out_shape=jax.ShapeDtypeStruct(adj_source.shape, f...  66.9 us
    unnamed x19, local copies, waits for them, and re-layouts  7.81 us

commit v1 on v0

--- a/solution.py
+++ b/solution.py
@@ -57,7 +57,8 @@
     columns[HALF:, 0] = real_low
     columns[:HALF, 1] = imag_coef
     columns[:, 2] = last
-    return split_table(forward), split_table(backward), columns
+    halves = [split_table(forward[:, part * HALF : (part + 1) * HALF]) for part in range(2)]
+    return np.stack(halves), split_table(backward), columns
 
 
 def product(table, value):
@@ -86,40 +87,68 @@
 
 
 def kernel(
-    adj, term, cap, cols, faces, forward, backward, coefs, blocks_hbm, out,
-    blk, turned, mat_high, mat_low, diag, recip, capacity, xsend, xrecv, wsend, wrecv,
-    total, ysend, yrecv, blk_sem, tm_sems, send_sems, recv_sems,
+    adj_hbm, term_hbm, cap_hbm, cols_hbm, faces_hbm, forward_hbm, backward_hbm, coefs_hbm,
+    blocks_hbm, out,
+    adj, term, cap, cols, faces, forward, backward, coefs, blk,
+    turned, mat_high, mat_low, diag, recip, capacity, psend, precv, pown, wsend, wrecv,
+    total, ysend, yrecv, load_sems, first_send, first_recv, last_sems, send_sems, recv_sems,
 ):
     group = lax.axis_index("tm")
     shard = lax.axis_index("space")
     shards = lax.axis_size("space")
     other = 1 - group
-    lower = lax.rem(shard + shards - 1, shards)
-    upper = lax.rem(shard + 1, shards)
+    has_lower = shard > 0
+    has_upper = shard < shards - 1
+    lower = jnp.maximum(shard - 1, 0)
+    upper = jnp.minimum(shard + 1, shards - 1)
     first = group == 0
 
-    blk_copy = pltpu.make_async_copy(blocks_hbm, blk, blk_sem)
-    blk_copy.start()
-
     barrier = pltpu.get_barrier_semaphore()
-    for target in ((other, shard), (group, lower), (group, upper)):
+
+    def greet(target):
         pl.semaphore_signal(barrier, inc=1, device_id=target, device_id_type=MESH)
-    case_0 = adj[:, 0, :]
-    case_1 = adj[:, 1, :]
-    xsend[...] = jnp.where(first, case_1, case_0)
-    mine = jnp.where(first, case_0, case_1)
-    pl.semaphore_wait(barrier, 3)
-
-    xcopy = pltpu.make_async_remote_copy(
-        src_ref=xsend, dst_ref=xrecv, send_sem=tm_sems.at[0], recv_sem=tm_sems.at[1],
-        device_id=(other, shard), device_id_type=MESH,
-    )
-    xcopy.start()
-
-    ids = [faces[i // 4, i % 4] for i in range(8)]
+
+    @pl.when(has_lower)
+    def _():
+        greet((0, lower))
+        greet((1, lower))
+
+    @pl.when(has_upper)
+    def _():
+        greet((0, upper))
+        greet((1, upper))
+
+    greet((other, shard))
+
+    loads = [
+        pltpu.make_async_copy(source, target, load_sems.at[i])
+        for i, (source, target) in enumerate(
+            [
+                (faces_hbm, faces), (cols_hbm, cols), (adj_hbm, adj), (term_hbm, term),
+                (cap_hbm, cap), (coefs_hbm, coefs), (forward_hbm, forward),
+                (blocks_hbm, blk), (backward_hbm, backward),
+            ]
+        )
+    ]
+    for load in loads:
+        load.start()
+
+    @pl.when(jnp.logical_not(has_lower))
+    def _():
+        wrecv[:, 0] = jnp.zeros_like(wrecv[:, 0])
+        precv[:, 0] = jnp.zeros_like(precv[:, 0])
+
+    @pl.when(jnp.logical_not(has_upper))
+    def _():
+        wrecv[:, 1] = jnp.zeros_like(wrecv[:, 1])
+        precv[:, 1] = jnp.zeros_like(precv[:, 1])
+
+    for load in loads:
+        load.wait()
+
+    ids = [faces[0, i // 4, i % 4] for i in range(8)]
     cap_row = cap[...]
     capacity[...] = reorder(jnp.broadcast_to(cap_row, (8, 8 * BLOCK)), ids)
-    blk_copy.wait()
     eye = lax.broadcasted_iota(jnp.int32, (BLOCK, BLOCK), 0) == lax.broadcasted_iota(
         jnp.int32, (BLOCK, BLOCK), 1
     )
@@ -147,45 +176,30 @@
             axis=0,
         )
 
-    def halo(slot):
-        down = pltpu.make_async_remote_copy(
-            src_ref=wsend.at[slot, 0], dst_ref=wrecv.at[slot, 1],
-            send_sem=send_sems.at[slot, 0], recv_sem=recv_sems.at[slot, 1],
-            device_id=(group, lower), device_id_type=MESH,
-        )
-        up = pltpu.make_async_remote_copy(
-            src_ref=wsend.at[slot, 1], dst_ref=wrecv.at[slot, 0],
-            send_sem=send_sems.at[slot, 1], recv_sem=recv_sems.at[slot, 0],
-            device_id=(group, upper), device_id_type=MESH,
-        )
-        return down, up
-
-    def send(slot, value):
-        wsend[slot, 0] = value[:, : 4 * BLOCK]
-        wsend[slot, 1] = value[:, 4 * BLOCK :]
-        down, up = halo(slot)
-        down.start()
-        up.start()
-
-    xcopy.wait()
-    theirs = xrecv[...]
-    source = jnp.concatenate(
-        [jnp.where(first, mine, theirs), jnp.where(first, theirs, mine)], axis=0
-    )
-    head = jnp.where(first, term[0:1, :], term[1:2, :]) * cap_row
-    row_ids = lax.broadcasted_iota(jnp.int32, (STEPS, 1), 0)
-    source = source + jnp.where(row_ids == 0, head, 0.0)
-    spectrum = reorder(product(forward[...], source), ids)
-    field = divided(spectrum)
-    send(0, field)
-    total[...] = jnp.zeros_like(total)
+    head_row = first & (lax.broadcasted_iota(jnp.int32, (HALF, 1), 0) == 0)
+    for case in range(2):
+        source = adj[:, case, :] + jnp.where(head_row, term[case : case + 1, :] * cap_row, 0.0)
+        part = divided(reorder(product(forward[group], source), ids))
+        psend[case, 0] = part[:, : 4 * BLOCK]
+        psend[case, 1] = part[:, 4 * BLOCK :]
+
+    def first_halo(side, case, sender):
+        return pltpu.make_async_remote_copy(
+            src_ref=psend.at[case, side], dst_ref=precv.at[sender, 1 - side],
+            send_sem=first_send.at[2 * side + case], recv_sem=first_recv.at[2 * (1 - side) + sender],
+            device_id=(case, upper if side else lower), device_id_type=MESH,
+        )
+
+    first_own = pltpu.make_async_remote_copy(
+        src_ref=psend.at[other], dst_ref=pown,
+        send_sem=first_send.at[4], recv_sem=first_recv.at[4],
+        device_id=(other, shard), device_id_type=MESH,
+    )
 
     lower_half = lax.broadcasted_iota(jnp.int32, (1, LANES), 1) < BLOCK
     turned_eye = lax.broadcasted_iota(jnp.int32, (BLOCK, LANES), 0) == lax.rem(
         lax.broadcasted_iota(jnp.int32, (BLOCK, LANES), 1), BLOCK
     )
-    no_lower = shard == 0
-    no_upper = shard == shards - 1
     for pair in range(4):
         left, right = ids[2 * pair], ids[2 * pair + 1]
         wanted = []
@@ -200,9 +214,9 @@
             if place < 8:
                 name = ids[place]
             elif place < 12:
-                name = jnp.where(no_lower, -1, place)
+                name = jnp.where(has_lower, place, -1)
             else:
-                name = jnp.where(no_upper, -1, place)
+                name = jnp.where(has_upper, place, -1)
             tile = jnp.where(wanted[0] == name, turned[0], 0.0)
             for k in range(1, 7):
                 tile = tile + jnp.where(wanted[k] == name, turned[k], 0.0)
@@ -211,6 +225,40 @@
             mat_high[where] = high
             mat_low[where] = low
 
+    neighbours = has_lower.astype(jnp.int32) + has_upper.astype(jnp.int32)
+    pl.semaphore_wait(barrier, 1 + 2 * neighbours)
+
+    @pl.when(has_lower)
+    def _():
+        for case in range(2):
+            first_halo(0, case, group).start()
+
+    @pl.when(has_upper)
+    def _():
+        for case in range(2):
+            first_halo(1, case, group).start()
+
+    first_own.start()
+
+    def halo(slot, side):
+        return pltpu.make_async_remote_copy(
+            src_ref=wsend.at[slot, side], dst_ref=wrecv.at[slot, 1 - side],
+            send_sem=send_sems.at[slot, side], recv_sem=recv_sems.at[slot, 1 - side],
+            device_id=(group, upper if side else lower), device_id_type=MESH,
+        )
+
+    def send(slot, value):
+        wsend[slot, 0] = value[:, : 4 * BLOCK]
+        wsend[slot, 1] = value[:, 4 * BLOCK :]
+
+        @pl.when(has_lower)
+        def _():
+            halo(slot, 0).start()
+
+        @pl.when(has_upper)
+        def _():
+            halo(slot, 1).start()
+
     def conduct(value, start, count):
         high, low = split(value)
         both = jnp.dot(
@@ -222,24 +270,50 @@
         )
         return both[:STEPS] + both[STEPS:] + rest
 
-    real_rows = row_ids <= HALF
+    real_rows = lax.broadcasted_iota(jnp.int32, (STEPS, 1), 0) <= HALF
     last = coefs[:, 2:3]
+
+    first_own.wait_recv()
+    value = jnp.concatenate([psend[group, 0] + pown[0], psend[group, 1] + pown[1]], axis=1)
+    total[...] = value
+    tail = jnp.sum(value * last, axis=0, keepdims=True)
+    result = conduct(value, 0, 8 * BLOCK)
+
+    @pl.when(has_lower)
+    def _():
+        for sender in range(2):
+            first_halo(1, 0, sender).wait_recv()
+
+    result = result + conduct(precv[0, 0] + precv[1, 0], 8 * BLOCK, 4 * BLOCK)
+
+    @pl.when(has_upper)
+    def _():
+        for sender in range(2):
+            first_halo(0, 0, sender).wait_recv()
+
+    result = result + conduct(precv[0, 1] + precv[1, 1], 12 * BLOCK, 4 * BLOCK)
+    send(0, divided(result))
 
     def round_of(slot, tail):
         value = jnp.concatenate([wsend[slot, 0], wsend[slot, 1]], axis=1)
         total[...] += value
         tail = tail + jnp.sum(value * last, axis=0, keepdims=True)
-        closes = lax.rem(slot, SWEEPS) == SWEEPS - 1
+        closes = lax.rem(slot + 1, SWEEPS) == SWEEPS - 1
         fix = jnp.where(closes, tail, 0.0) * capacity[0:1, :]
         tail = jnp.where(closes, 0.0, tail)
         result = conduct(value, 0, 8 * BLOCK) - jnp.where(real_rows, fix, 0.0)
-        down, up = halo(slot)
-        up.wait_recv()
+
+        @pl.when(has_lower)
+        def _():
+            halo(slot, 1).wait_recv()
+
         result = result + conduct(wrecv[slot, 0], 8 * BLOCK, 4 * BLOCK)
-        down.wait_recv()
+
+        @pl.when(has_upper)
+        def _():
+            halo(slot, 0).wait_recv()
+
         result = result + conduct(wrecv[slot, 1], 12 * BLOCK, 4 * BLOCK)
-        down.wait_send()
-        up.wait_send()
         return divided(result), tail
 
     def step(slot, tail):
@@ -247,8 +321,8 @@
         send(slot + 1, value)
         return tail
 
-    tail = lax.fori_loop(0, ROUNDS - 1, step, jnp.zeros((1, 8 * BLOCK), jnp.float32))
-    value, _ = round_of(ROUNDS - 1, tail)
+    tail = lax.fori_loop(0, ROUNDS - 2, step, tail)
+    value, _ = round_of(ROUNDS - 2, tail)
 
     places = []
     for block in range(8):
@@ -260,10 +334,27 @@
     early, late = summed[:HALF], summed[HALF:]
     ysend[...] = jnp.where(first, late, early)
     ycopy = pltpu.make_async_remote_copy(
-        src_ref=ysend, dst_ref=yrecv, send_sem=tm_sems.at[2], recv_sem=tm_sems.at[3],
+        src_ref=ysend, dst_ref=yrecv, send_sem=last_sems.at[0], recv_sem=last_sems.at[1],
         device_id=(other, shard), device_id_type=MESH,
     )
     ycopy.start()
+
+    first_own.wait_send()
+
+    @pl.when(has_lower)
+    def _():
+        for case in range(2):
+            first_halo(0, case, group).wait_send()
+        for slot in range(ROUNDS - 1):
+            halo(slot, 0).wait_send()
+
+    @pl.when(has_upper)
+    def _():
+        for case in range(2):
+            first_halo(1, case, group).wait_send()
+        for slot in range(ROUNDS - 1):
+            halo(slot, 1).wait_send()
+
     kept = jnp.where(first, early, late)
     ycopy.wait()
     came = yrecv[...]
@@ -274,15 +365,23 @@
 def per_device(adj_source, terminal, capacity, blocks, columns, face_lists):
     nodes = capacity.shape[0]
     forward, backward, coefs = tables()
-    vmem = pl.BlockSpec(memory_space=pltpu.VMEM)
-    smem = pl.BlockSpec(memory_space=pltpu.SMEM)
-    f32, bf16 = jnp.float32, jnp.bfloat16
+    hbm = pl.BlockSpec(memory_space=pltpu.HBM)
+    f32, bf16, i32 = jnp.float32, jnp.bfloat16, jnp.int32
+    dma = pltpu.SemaphoreType.DMA
     return pl.pallas_call(
         kernel,
         out_shape=jax.ShapeDtypeStruct(adj_source.shape, f32),
-        in_specs=[vmem, vmem, vmem, smem, smem, vmem, vmem, vmem, pl.BlockSpec(memory_space=pl.ANY)],
-        out_specs=vmem,
+        in_specs=[hbm] * 9,
+        out_specs=pl.BlockSpec(memory_space=pltpu.VMEM),
         scratch_shapes=[
+            pltpu.VMEM(adj_source.shape, f32),
+            pltpu.VMEM(terminal.shape, f32),
+            pltpu.VMEM((1, nodes), f32),
+            pltpu.SMEM(columns.shape, i32),
+            pltpu.SMEM(face_lists.shape, i32),
+            pltpu.VMEM(forward.shape, bf16),
+            pltpu.VMEM(backward.shape, bf16),
+            pltpu.VMEM(coefs.shape, f32),
             pltpu.VMEM(blocks.shape, f32),
             pltpu.VMEM((7, BLOCK, LANES), f32),
             pltpu.VMEM((16 * BLOCK, nodes), bf16),
@@ -290,24 +389,27 @@
             pltpu.VMEM((8, nodes), f32),
             pltpu.VMEM((3, HALF, nodes), f32),
             pltpu.VMEM((8, nodes), f32),
-            pltpu.VMEM((HALF, nodes), f32),
-            pltpu.VMEM((HALF, nodes), f32),
-            pltpu.VMEM((ROUNDS, 2, STEPS, nodes // 2), f32),
-            pltpu.VMEM((ROUNDS, 2, STEPS, nodes // 2), f32),
+            pltpu.VMEM((2, 2, STEPS, nodes // 2), f32),
+            pltpu.VMEM((2, 2, STEPS, nodes // 2), f32),
+            pltpu.VMEM((2, STEPS, nodes // 2), f32),
+            pltpu.VMEM((ROUNDS - 1, 2, STEPS, nodes // 2), f32),
+            pltpu.VMEM((ROUNDS - 1, 2, STEPS, nodes // 2), f32),
             pltpu.VMEM((STEPS, nodes), f32),
             pltpu.VMEM((HALF, nodes), f32),
             pltpu.VMEM((HALF, nodes), f32),
-            pltpu.SemaphoreType.DMA,
-            pltpu.SemaphoreType.DMA((4,)),
-            pltpu.SemaphoreType.DMA((ROUNDS, 2)),
-            pltpu.SemaphoreType.DMA((ROUNDS, 2)),
+            dma((9,)),
+            dma((5,)),
+            dma((5,)),
+            dma((2,)),
+            dma((ROUNDS - 1, 2)),
+            dma((ROUNDS - 1, 2)),
         ],
         compiler_params=pltpu.CompilerParams(
-            collective_id=0, has_side_effects=True, vmem_limit_bytes=24 * 1024 * 1024
+            collective_id=0, has_side_effects=True, vmem_limit_bytes=60 * 1024 * 1024
         ),
         name="window",
     )(
-        adj_source, terminal, capacity.reshape(1, nodes), columns, face_lists.reshape(2, 4),
+        adj_source, terminal, capacity.reshape(1, nodes), columns, face_lists,
         jnp.asarray(forward), jnp.asarray(backward), jnp.asarray(coefs), blocks,
     )
 

time: 75.2 us -> 57.6 us (0.77)
  the two profiles are of different devices: /device:TPU:1 before, /device:TPU:257 now
where the time goes in v1:
time: 57.6 us; the launch traced here: 57.4 us
  Pallas kernels  55.9 us (97%)
  local copies, waits for them, and re-layouts  1.47 us (3%)
    pallas_call x1, Pallas kernels, per_device(): pl.pallas_call(kernel, out_shape=jax.ShapeDtypeStruct(adj_source.shape, f...  55.9 us
    unnamed x1, local copies, waits for them, and re-layouts  1.47 us

profile of v1, /device:TPU:257, one launch (start us, length us, event | category | flops | bytes accessed | tf_op | source)
XLA Modules:
  0.0 57.4 jit_solution(15419771453757153066)
XLA Ops:
  0.0 55.9 %window.1 = f32[16,2,512]{2,1,0:T(2,128)} custom-call(f32[16,2,512]{2,1,0:T(2,128)} %adj_hbm.1, f32[2,512]{1,0:T(2,128)} %term_hbm.1, f32[1,512]{1,0:T(1,128)} %bitcast.1, s32[8,7]{1,0:T(8,128)} %cols_hbm.1, s32[1,2,4]{2,1,0:T(2,128)} %faces_hbm.1, bf16[2,32,48]{2,1,0:T(8,128)(2,1)} %constant.6.clone.forward_hbm, bf16[32,96]{1,0:T(8,128)(2,1)} %constant.7.clone.backward_hbm, ...), custom_call_target="tpu_custom_call" | custom-call | tf_op jit(solution)/shard_map/window/pallas_call | solution.py:371
  55.9 1.5 %copy.11 = f32[16,2,512]{2,1,0:T(2,128)} copy(f32[16,2,512]{2,1,0:T(2,128)} %window.1) | data formatting | bytes 131072

commit v2 on v1

v2 whole, which is shorter than its diff:
```python
import functools
import math

import jax
import jax.numpy as jnp
import numpy as np
from jax import lax
from jax.experimental import pallas as pl
from jax.experimental.pallas import tpu as pltpu
from jax.sharding import PartitionSpec as P

OUTER = 3
SWEEPS = 3
STEPS = 32
HALF = STEPS // 2
CORNER_WEIGHT = 0.1
ROOT = CORNER_WEIGHT ** (1.0 / STEPS)
PAIRS = (OUTER * SWEEPS - 3) // 2
BLOCK = 64
LANES = 128
MESH = pl.DeviceIdType.MESH


def split(value):
    high = value.astype(jnp.bfloat16)
    low = (value - high.astype(jnp.float32)).astype(jnp.bfloat16)
    return high, low


def split_table(table):
    high = table.astype(jnp.bfloat16)
    low = (table - high.astype(np.float64)).astype(jnp.bfloat16)
    return np.concatenate([high, high, low], axis=1)


def tables():
    steps = np.arange(STEPS)
    modes = np.arange(HALF)
    angles = 2.0 * np.pi * ((modes[:, None] * steps[None, :]) % STEPS) / STEPS
    nyquist = (-1.0) ** steps
    cosines, sines = np.cos(angles), -np.sin(angles)
    sines[0] = nyquist
    basis = np.concatenate([cosines, sines], axis=0)
    scale = CORNER_WEIGHT ** (steps / STEPS)
    forward = basis * scale[None, :]
    weight = np.full((STEPS,), 2.0)
    weight[0] = weight[HALF] = 1.0
    inverse = (basis * weight[:, None]).T / STEPS
    last = inverse[STEPS - 1] * ROOT
    backward = inverse / scale[:, None]
    real_coef = 1.0 - ROOT * np.cos(2.0 * np.pi * modes / STEPS)
    imag_coef = ROOT * np.sin(2.0 * np.pi * modes / STEPS)
    real_low = real_coef.copy()
    real_low[0] = 1.0 + ROOT
    columns = np.zeros((STEPS, LANES), np.float32)
    columns[:HALF, 0] = real_coef
    columns[HALF:, 0] = real_low
    columns[:HALF, 1] = imag_coef
    columns[:, 2] = last
    halves = [split_table(forward[:, part * HALF : (part + 1) * HALF]) for part in range(2)]
    return np.stack(halves), split_table(backward), columns


def product(table, value):
    high, low = split(value)
    return jnp.dot(
        table, jnp.concatenate([high, low, high], axis=0), preferred_element_type=jnp.float32
    )


def reorder(value, ids):
    lower_half = lax.broadcasted_iota(jnp.int32, (1, LANES), 1) < BLOCK
    both = []
    for tile in range(4):
        plain = value[:, tile * LANES : (tile + 1) * LANES]
        turned = pltpu.roll(plain, BLOCK, 1)
        both.append(jnp.where(lower_half, plain, turned))
        both.append(jnp.where(lower_half, turned, plain))
    tiles = []
    for tile in range(4):
        wanted = jnp.where(lower_half, ids[2 * tile], ids[2 * tile + 1])
        total = both[0]
        for block in range(1, 8):
            total = jnp.where(wanted == block, both[block], total)
        tiles.append(total)
    return jnp.concatenate(tiles, axis=1)


def kernel(
    adj_hbm, term_hbm, cap_hbm, cols_hbm, faces_hbm, forward_hbm, backward_hbm, coefs_hbm,
    blocks_hbm, out,
    adj, term, cap, cols, faces, forward, backward, coefs, blk,
    turned, names, mat_high, mat_low, face_high, face_low, diag, recip, face_recip, capacity,
    meta, met, tiles, psend, precv, pown, wsend, near, far, own_part, part, total, ysend, yrecv,
    load_sems, first_send, first_recv, once_send, once_recv, last_sems, send_sems, recv_sems,
):
    group = lax.axis_index("tm")
    shard = lax.axis_index("space")
    shards = lax.axis_size("space")
    other = 1 - group
    first = group == 0
    has = (shard > 0, shard < shards - 1)
    has_far = (shard > 1, shard < shards - 2)
    beside = (jnp.maximum(shard - 1, 0), jnp.minimum(shard + 1, shards - 1))
    beyond = (jnp.maximum(shard - 2, 0), jnp.minimum(shard + 2, shards - 1))

    barrier = pltpu.get_barrier_semaphore()

    def greet(target):
        pl.semaphore_signal(barrier, inc=1, device_id=target, device_id_type=MESH)

    greets = 1
    for side in range(2):

        @pl.when(has_far[side])
        def _():
            greet((group, beyond[side]))

        @pl.when(has[side])
        def _():
            greet((0, beside[side]))
            greet((1, beside[side]))

        greets = greets + 2 * has[side].astype(jnp.int32) + has_far[side].astype(jnp.int32)

    greet((other, shard))

    loads = [
        pltpu.make_async_copy(source, target, load_sems.at[i])
        for i, (source, target) in enumerate(
            [
                (faces_hbm, faces), (cols_hbm, cols), (adj_hbm, adj), (term_hbm, term),
                (cap_hbm, cap), (coefs_hbm, coefs), (forward_hbm, forward),
                (blocks_hbm, blk), (backward_hbm, backward),
            ]
        )
    ]
    for load in loads:
        load.start()

    for side in range(2):

        @pl.when(jnp.logical_not(has_far[side]))
        def _():
            far[:, side] = jnp.zeros_like(far[:, side])

        @pl.when(jnp.logical_not(has[side]))
        def _():
            near[:, side] = jnp.zeros_like(near[:, side])
            part[:, side] = jnp.zeros_like(part[:, side])
            precv[:, side] = jnp.zeros_like(precv[:, side])
            tiles[side] = jnp.zeros_like(tiles[side])
            met[side] = jnp.ones_like(met[side])

    for load in loads:
        load.wait()

    ids = [faces[0, i // 4, i % 4] for i in range(8)]
    cap_row = cap[...]
    capacity[...] = reorder(jnp.broadcast_to(cap_row, (8, 8 * BLOCK)), ids)
    eye = lax.broadcasted_iota(jnp.int32, (BLOCK, BLOCK), 0) == lax.broadcasted_iota(
        jnp.int32, (BLOCK, BLOCK), 1
    )
    rows = [
        jnp.sum(jnp.where(eye, blk[ids[i], 0], 0.0), axis=0, keepdims=True) for i in range(8)
    ]
    diag[...] = jnp.broadcast_to(jnp.concatenate(rows, axis=1), diag.shape)

    def reciprocals(cap_own, diag_own):
        imag = coefs[0:HALF, 1:2] * cap_own
        found = []
        for half in range(2):
            real = coefs[half * HALF : (half + 1) * HALF, 0:1] * cap_own + diag_own
            over = 1.0 / (real * real + imag * imag)
            found.append(real * over)
            if half == 0:
                turn = -imag * over
        return found[0], found[1], turn

    def divide(value, upper_real, lower_real, turn):
        upper_part, lower_part = value[:HALF], value[HALF:]
        return jnp.concatenate(
            [
                upper_real * upper_part - turn * lower_part,
                turn * upper_part + lower_real * lower_part,
            ],
            axis=0,
        )

    recip[0], recip[1], recip[2] = reciprocals(capacity[0:1, :], diag[0:1, :])

    def divided(value):
        return divide(value, recip[0], recip[1], recip[2])

    head_row = first & (lax.broadcasted_iota(jnp.int32, (HALF, 1), 0) == 0)
    for case in range(2):
        source = adj[:, case, :] + jnp.where(head_row, term[case : case + 1, :] * cap_row, 0.0)
        field = divided(reorder(product(forward[group], source), ids))
        psend[case, 0] = field[:, : 4 * BLOCK]
        psend[case, 1] = field[:, 4 * BLOCK :]

    lower_half = lax.broadcasted_iota(jnp.int32, (1, LANES), 1) < BLOCK
    turned_eye = lax.broadcasted_iota(jnp.int32, (BLOCK, LANES), 0) == lax.rem(
        lax.broadcasted_iota(jnp.int32, (BLOCK, LANES), 1), BLOCK
    )
    for pair in range(4):
        left, right = ids[2 * pair], ids[2 * pair + 1]
        for k in range(7):
            entry = jnp.concatenate([blk[left, k], blk[right, k]], axis=0)
            entry = -entry.T
            if k == 0:
                entry = jnp.where(turned_eye, 0.0, entry)
            turned[pair, k] = entry
            names[8 * pair + k : 8 * pair + k + 1, :] = jnp.where(
                lower_half, cols[left, k], cols[right, k]
            )
        names[8 * pair + 7 : 8 * pair + 8, :] = jnp.full((1, LANES), -1, jnp.int32)
    raw = names[...]
    place_of = jnp.zeros_like(raw)
    for i in range(8):
        place_of = jnp.where(raw == ids[i], i, place_of)
    place_of = jnp.where(raw >= 8, jnp.where(has[0], raw, -1), place_of)
    place_of = jnp.where(raw >= 12, jnp.where(has[1], raw, -1), place_of)
    named = place_of.astype(jnp.float32)
    for side in range(2):
        meta[side, 0:16] = named[16 * side : 16 * side + 16]
        for row, table in ((16, capacity), (24, diag)):
            for pair in range(2):
                lane = (2 * side + pair) * LANES
                meta[side, row + 4 * pair : row + 4 * pair + 4] = table[0:4, lane : lane + LANES]
    for pair in range(4):
        wanted = [named[8 * pair + k : 8 * pair + k + 1] for k in range(7)]

        def build(place, carry, pair=pair, wanted=wanted):
            name = place.astype(jnp.float32)
            tile = jnp.where(wanted[0] == name, turned[pair, 0], 0.0)
            for k in range(1, 7):
                tile = tile + jnp.where(wanted[k] == name, turned[pair, k], 0.0)
            high, low = split(tile)
            at = pl.ds(pl.multiple_of(place * BLOCK, BLOCK), BLOCK)
            mat_high[at, pair * LANES : (pair + 1) * LANES] = high
            mat_low[at, pair * LANES : (pair + 1) * LANES] = low
            return carry

        lax.fori_loop(0, 16, build, 0)

    pl.semaphore_wait(barrier, greets)

    def remote(source, target, send_sem, recv_sem, device):
        return pltpu.make_async_remote_copy(
            src_ref=source, dst_ref=target, send_sem=send_sem, recv_sem=recv_sem,
            device_id=device, device_id_type=MESH,
        )

    def first_halo(side, case, sender):
        return remote(
            psend.at[case, side], precv.at[sender, 1 - side],
            first_send.at[2 * side + case], first_recv.at[2 * (1 - side) + sender],
            (case, beside[side]),
        )

    first_own = remote(
        psend.at[other], pown, first_send.at[4], first_recv.at[4], (other, shard)
    )

    def matrix_rows(side):
        return remote(
            turned.at[2 * side + group, pl.ds(1, 6)], tiles.at[1 - side, group],
            once_send.at[side], once_recv.at[1 - side], (group, beside[side]),
        )

    def row_facts(side):
        return remote(
            meta.at[side], met.at[1 - side],
            once_send.at[2 + side], once_recv.at[3 - side], (group, beside[side]),
        )

    def passed_on(side):
        return remote(
            tiles.at[side, group], tiles.at[side, group],
            once_send.at[4 + side], once_recv.at[4 + side], (other, shard),
        )

    def field_near(slot, side):
        return remote(
            wsend.at[slot, side], near.at[slot, 1 - side],
            send_sems.at[slot, side], recv_sems.at[slot, 1 - side], (group, beside[side]),
        )

    def field_far(slot, side):
        return remote(
            wsend.at[slot, side], far.at[slot, 1 - side],
            send_sems.at[slot, 2 + side], recv_sems.at[slot, 3 - side], (group, beyond[side]),
        )

    def part_near(slot, side):
        return remote(
            own_part.at[slot, side], part.at[slot, 1 - side],
            send_sems.at[slot, 4 + side], recv_sems.at[slot, 5 - side], (group, beside[side]),
        )

    for side in range(2):

        @pl.when(has[side])
        def _():
            for case in range(2):
                first_halo(side, case, group).start()

    first_own.start()
    for side in range(2):

        @pl.when(has[side])
        def _():
            row_facts(side).start()
            matrix_rows(side).start()

    def times(value, matrix_high, matrix_low):
        high, low = split(value)
        both = jnp.dot(
            jnp.concatenate([high, low], axis=0), matrix_high, preferred_element_type=jnp.float32
        )
        rest = jnp.dot(high, matrix_low, preferred_element_type=jnp.float32)
        return both[:STEPS] + both[STEPS:] + rest

    def conduct(value, start, count):
        return times(
            value, mat_high[start : start + count, :], mat_low[start : start + count, :]
        )

    def face(value, side, start):
        return times(
            value, face_high[side, start : start + 4 * BLOCK], face_low[side, start : start + 4 * BLOCK]
        )

    real_rows = lax.broadcasted_iota(jnp.int32, (STEPS, 1), 0) <= HALF
    last = coefs[:, 2:3]

    def own_product(value, tail, application):
        total[...] += value
        tail = tail + jnp.sum(value * last, axis=0, keepdims=True)
        closes = lax.rem(application, SWEEPS) == SWEEPS - 1
        fix = jnp.where(closes, tail, 0.0) * capacity[0:1, :]
        tail = jnp.where(closes, 0.0, tail)
        return conduct(value, 0, 8 * BLOCK) - jnp.where(real_rows, fix, 0.0), tail

    def advance(slot, value, tail):
        wsend[slot, 0] = value[:, : 4 * BLOCK]
        wsend[slot, 1] = value[:, 4 * BLOCK :]
        paired = slot < PAIRS
        for side in range(2):

            @pl.when(has_far[side] & paired)
            def _():
                field_far(slot, side).start()

        for side in range(2):

            @pl.when(has[side])
            def _():
                field_near(slot, side).start()

        result, tail = own_product(value, tail, 2 * slot + 1)
        own_part[slot, 0] = result[:, : 4 * BLOCK]
        own_part[slot, 1] = result[:, 4 * BLOCK :]
        for side in range(2):

            @pl.when(has[side] & paired)
            def _():
                part_near(slot, side).start()

        return tail

    first_own.wait_recv()
    value = jnp.concatenate([psend[group, 0] + pown[0], psend[group, 1] + pown[1]], axis=1)
    total[...] = jnp.zeros_like(total)
    result, tail = own_product(value, jnp.zeros((1, 8 * BLOCK), jnp.float32), jnp.int32(0))
    for side in range(2):

        @pl.when(has[side])
        def _():
            for sender in range(2):
                first_halo(1 - side, 0, sender).wait_recv()

        result = result + conduct(
            precv[0, side] + precv[1, side], (8 + 4 * side) * BLOCK, 4 * BLOCK
        )
    tail = advance(jnp.int32(0), divided(result), tail)

    for side in range(2):

        @pl.when(has[side])
        def _():
            matrix_rows(1 - side).wait_recv()
            passed_on(side).start()

    for side in range(2):

        @pl.when(has[side])
        def _():
            row_facts(1 - side).wait_recv()

        face_recip[side, 0], face_recip[side, 1], face_recip[side, 2] = reciprocals(
            jnp.concatenate([met[side, 16:17], met[side, 20:21]], axis=1),
            jnp.concatenate([met[side, 24:25], met[side, 28:29]], axis=1),
        )

        @pl.when(has[side])
        def _():
            passed_on(side).wait_recv()

        for pair in range(2):

            def build(place, carry, side=side, pair=pair):
                name = (place + 8).astype(jnp.float32)
                tile = jnp.where(
                    met[side, 8 * pair + 1 : 8 * pair + 2] == name, tiles[side, pair, 0], 0.0
                )
                for k in range(2, 7):
                    wanted = met[side, 8 * pair + k : 8 * pair + k + 1]
                    tile = tile + jnp.where(wanted == name, tiles[side, pair, k - 1], 0.0)
                high, low = split(tile)
                at = pl.ds(pl.multiple_of(place * BLOCK, BLOCK), BLOCK)
                face_high[side, at, pair * LANES : (pair + 1) * LANES] = high
                face_low[side, at, pair * LANES : (pair + 1) * LANES] = low
                return carry

            lax.fori_loop(0, 8, build, 0)

    def couple(slot, tail):
        faces_of = [face(wsend[slot, side], side, 4 * (1 - side) * BLOCK) for side in range(2)]
        result = jnp.concatenate([own_part[slot, 0], own_part[slot, 1]], axis=1)
        for side in range(2):

            @pl.when(has[side])
            def _():
                field_near(slot, 1 - side).wait_recv()

            result = result + conduct(near[slot, side], (8 + 4 * side) * BLOCK, 4 * BLOCK)
        result, tail = own_product(divided(result), tail, 2 * slot + 2)
        for side in range(2):

            @pl.when(has_far[side])
            def _():
                field_far(slot, 1 - side).wait_recv()

            ahead = faces_of[side] + face(far[slot, side], side, 4 * side * BLOCK)

            @pl.when(has[side])
            def _():
                part_near(slot, 1 - side).wait_recv()

            ahead = divide(
                ahead + part[slot, side],
                face_recip[side, 0], face_recip[side, 1], face_recip[side, 2],
            )
            result = result + conduct(ahead, (8 + 4 * side) * BLOCK, 4 * BLOCK)
        return advance(slot + 1, divided(result), tail)

    lax.fori_loop(0, PAIRS, couple, tail)

    result = jnp.concatenate([own_part[PAIRS, 0], own_part[PAIRS, 1]], axis=1)
    for side in range(2):

        @pl.when(has[side])
        def _():
            field_near(PAIRS, 1 - side).wait_recv()

        result = result + conduct(near[PAIRS, side], (8 + 4 * side) * BLOCK, 4 * BLOCK)
    value = divided(result)

    places = []
    for block in range(8):
        place = jnp.int32(0)
        for i in range(1, 8):
            place = place + jnp.where(ids[i] == block, i, 0)
        places.append(place)
    summed = product(backward[...], reorder(total[...] + value, places))
    early, late = summed[:HALF], summed[HALF:]
    ysend[...] = jnp.where(first, late, early)
    ycopy = remote(ysend, yrecv, last_sems.at[0], last_sems.at[1], (other, shard))
    ycopy.start()

    first_own.wait_send()
    for side in range(2):

        @pl.when(has[side])
        def _():
            for case in range(2):
                first_halo(side, case, group).wait_send()
            matrix_rows(side).wait_send()
            row_facts(side).wait_send()
            passed_on(side).wait_send()
            for slot in range(PAIRS + 1):
                field_near(slot, side).wait_send()
            for slot in range(PAIRS):
                part_near(slot, side).wait_send()

        @pl.when(has_far[side])
        def _():
            for slot in range(PAIRS):
                field_far(slot, side).wait_send()

    kept = jnp.where(first, early, late)
    ycopy.wait()
    came = yrecv[...]
    out[:, 0, :] = jnp.where(first, kept, came)
    out[:, 1, :] = jnp.where(first, came, kept)


def per_device(adj_source, terminal, capacity, blocks, columns, face_lists):
    nodes = capacity.shape[0]
    half = nodes // 2
    forward, backward, coefs = tables()
    hbm = pl.BlockSpec(memory_space=pltpu.HBM)
    f32, bf16, i32 = jnp.float32, jnp.bfloat16, jnp.int32
    dma = pltpu.SemaphoreType.DMA
    return pl.pallas_call(
        kernel,
        out_shape=pltpu.VMEM(adj_source.shape, f32),
        in_specs=[hbm] * 9,
        out_specs=pl.BlockSpec(memory_space=pltpu.VMEM),
        scratch_shapes=[
            pltpu.VMEM(adj_source.shape, f32),
            pltpu.VMEM(terminal.shape, f32),
            pltpu.VMEM((1, nodes), f32),
            pltpu.SMEM(columns.shape, i32),
            pltpu.SMEM(face_lists.shape, i32),
            pltpu.VMEM(forward.shape, bf16),
            pltpu.VMEM(backward.shape, bf16),
            pltpu.VMEM(coefs.shape, f32),
            pltpu.VMEM(blocks.shape, f32),
            pltpu.VMEM((4, 7, BLOCK, LANES), f32),
            pltpu.VMEM((32, LANES), i32),
            pltpu.VMEM((16 * BLOCK, nodes), bf16),
            pltpu.VMEM((16 * BLOCK, nodes), bf16),
            pltpu.VMEM((2, 8 * BLOCK, half), bf16),
            pltpu.VMEM((2, 8 * BLOCK, half), bf16),
            pltpu.VMEM((8, nodes), f32),
            pltpu.VMEM((3, HALF, nodes), f32),
            pltpu.VMEM((2, 3, HALF, half), f32),
            pltpu.VMEM((8, nodes), f32),
            pltpu.VMEM((2, 32, LANES), f32),
            pltpu.VMEM((2, 32, LANES), f32),
            pltpu.VMEM((2, 2, 6, BLOCK, LANES), f32),
            pltpu.VMEM((2, 2, STEPS, half), f32),
            pltpu.VMEM((2, 2, STEPS, half), f32),
            pltpu.VMEM((2, STEPS, half), f32),
            pltpu.VMEM((PAIRS + 1, 2, STEPS, half), f32),
            pltpu.VMEM((PAIRS + 1, 2, STEPS, half), f32),
            pltpu.VMEM((PAIRS + 1, 2, STEPS, half), f32),
            pltpu.VMEM((PAIRS + 1, 2, STEPS, half), f32),
            pltpu.VMEM((PAIRS + 1, 2, STEPS, half), f32),
            pltpu.VMEM((STEPS, nodes), f32),
            pltpu.VMEM((HALF, nodes), f32),
            pltpu.VMEM((HALF, nodes), f32),
            dma((9,)),
            dma((5,)),
            dma((5,)),
            dma((6,)),
            dma((6,)),
            dma((2,)),
            dma((PAIRS + 1, 6)),
            dma((PAIRS + 1, 6)),
        ],
        compiler_params=pltpu.CompilerParams(
            collective_id=0, has_side_effects=True, vmem_limit_bytes=60 * 1024 * 1024
        ),
        name="window",
    )(
        adj_source, terminal, capacity.reshape(1, nodes), columns, face_lists,
        jnp.asarray(forward), jnp.asarray(backward), jnp.asarray(coefs), blocks,
    )


def solution(mesh):
    return jax.shard_map(
        per_device,
        mesh=mesh,
        in_specs=(
            P("tm", None, "space"),
            P(None, "space"),
            P("space"),
            P("space", None, None, None),
            P("space", None),
            P("space", None, None),
        ),
        out_specs=P("tm", None, "space"),
        check_vma=False,
    )
```

time: 57.6 us -> 45.3 us (0.79)
  Pallas kernels: 55.9 us -> 44.5 us
  local copies, waits for them, and re-layouts: 1.47 us -> 0.63 us
    pallas_call x1, Pallas kernels: 55.9 us -> 44.5 us  [per_device(): pl.pallas_call(kernel, out_shape=pltpu.VMEM(adj_source.shape, f32), in_sp...]
    unnamed x1, local copies, waits for them, and re-layouts: 1.47 us -> 0.63 us
where the time goes in v2:
time: 45.3 us; the launch traced here: 45.2 us
  Pallas kernels  44.5 us (98%)
  local copies, waits for them, and re-layouts  0.63 us (1%)
    pallas_call x1, Pallas kernels, per_device(): pl.pallas_call(kernel, out_shape=pltpu.VMEM(adj_source.shape, f32), in_sp...  44.5 us

profile of v2, /device:TPU:257, one launch (start us, length us, event | category | flops | bytes accessed | tf_op | source)
XLA Modules:
  0.0 45.2 jit_solution(13629488279551944801)
XLA Ops:
  0.0 44.5 %window.1 = f32[16,2,512]{2,1,0:T(2,128)S(1)} custom-call(f32[16,2,512]{2,1,0:T(2,128)} %adj_hbm.1, f32[2,512]{1,0:T(2,128)} %term_hbm.1, f32[1,512]{1,0:T(1,128)} %bitcast.1, s32[8,7]{1,0:T(8,128)} %cols_hbm.1, s32[1,2,4]{2,1,0:T(2,128)} %faces_hbm.1, bf16[2,32,48]{2,1,0:T(8,128)(2,1)} %constant.6.clone.forward_hbm, ...), custom_call_target="tpu_custom_call" | custom-call | tf_op jit(solution)/shard_map/window/pallas_call | solution.py:517
  44.5 0.6 %copy.11 = f32[16,2,512]{2,1,0:T(2,128)} copy(f32[16,2,512]{2,1,0:T(2,128)S(1)} %window.1) | data formatting | bytes 131072

commit v3 on v2

--- a/solution.py
+++ b/solution.py
@@ -91,7 +91,7 @@
     blocks_hbm, out,
     adj, term, cap, cols, faces, forward, backward, coefs, blk,
     turned, names, mat_high, mat_low, face_high, face_low, diag, recip, face_recip, capacity,
-    meta, met, tiles, psend, precv, pown, wsend, near, far, own_part, part, total, ysend, yrecv,
+    meta, met, tiles, psend, precv, pown, wsend, near, far, own_part, part_send, part, total, ysend, yrecv,
     load_sems, first_send, first_recv, once_send, once_recv, last_sems, send_sems, recv_sems,
 ):
     group = lax.axis_index("tm")
@@ -295,7 +295,7 @@
 
     def part_near(slot, side):
         return remote(
-            own_part.at[slot, side], part.at[slot, 1 - side],
+            part_send.at[slot, side], part.at[slot, 1 - side],
             send_sems.at[slot, 4 + side], recv_sems.at[slot, 5 - side], (group, beside[side]),
         )
 
@@ -307,12 +307,6 @@
                 first_halo(side, case, group).start()
 
     first_own.start()
-    for side in range(2):
-
-        @pl.when(has[side])
-        def _():
-            row_facts(side).start()
-            matrix_rows(side).start()
 
     def times(value, matrix_high, matrix_low):
         high, low = split(value)
@@ -326,6 +320,9 @@
         return times(
             value, mat_high[start : start + count, :], mat_low[start : start + count, :]
         )
+
+    def received(from_lower, from_upper):
+        return conduct(jnp.concatenate([from_lower, from_upper], axis=1), 8 * BLOCK, 8 * BLOCK)
 
     def face(value, side, start):
         return times(
@@ -343,32 +340,44 @@
         tail = jnp.where(closes, 0.0, tail)
         return conduct(value, 0, 8 * BLOCK) - jnp.where(real_rows, fix, 0.0), tail
 
-    def advance(slot, value, tail):
+    def advance(slot, value, tail, application, paired):
         wsend[slot, 0] = value[:, : 4 * BLOCK]
         wsend[slot, 1] = value[:, 4 * BLOCK :]
-        paired = slot < PAIRS
-        for side in range(2):
-
-            @pl.when(has_far[side] & paired)
-            def _():
-                field_far(slot, side).start()
-
         for side in range(2):
 
             @pl.when(has[side])
             def _():
                 field_near(slot, side).start()
 
-        result, tail = own_product(value, tail, 2 * slot + 1)
-        own_part[slot, 0] = result[:, : 4 * BLOCK]
-        own_part[slot, 1] = result[:, 4 * BLOCK :]
+        if paired:
+            for side in range(2):
+
+                @pl.when(has_far[side])
+                def _():
+                    field_far(slot, side).start()
+
+        result, tail = own_product(value, tail, application)
+        own_part[slot] = result
+        if paired:
+            result = divided(result)
+            part_send[slot, 0] = result[:, : 4 * BLOCK]
+            part_send[slot, 1] = result[:, 4 * BLOCK :]
+            for side in range(2):
+
+                @pl.when(has[side])
+                def _():
+                    part_near(slot, side).start()
+
+        return tail
+
+    def first_step(slot):
         for side in range(2):
 
-            @pl.when(has[side] & paired)
+            @pl.when(has[side])
             def _():
-                part_near(slot, side).start()
-
-        return tail
+                field_near(slot, 1 - side).wait_recv()
+
+        return divided(own_part[slot] + received(near[slot, 0], near[slot, 1]))
 
     first_own.wait_recv()
     value = jnp.concatenate([psend[group, 0] + pown[0], psend[group, 1] + pown[1]], axis=1)
@@ -378,13 +387,18 @@
 
         @pl.when(has[side])
         def _():
+            row_facts(side).start()
+            matrix_rows(side).start()
+
+    for side in range(2):
+
+        @pl.when(has[side])
+        def _():
             for sender in range(2):
                 first_halo(1 - side, 0, sender).wait_recv()
 
-        result = result + conduct(
-            precv[0, side] + precv[1, side], (8 + 4 * side) * BLOCK, 4 * BLOCK
-        )
-    tail = advance(jnp.int32(0), divided(result), tail)
+    result = result + received(precv[0, 0] + precv[1, 0], precv[0, 1] + precv[1, 1])
+    tail = advance(0, divided(result), tail, jnp.int32(1), False)
 
     for side in range(2):
 
@@ -392,6 +406,8 @@
         def _():
             matrix_rows(1 - side).wait_recv()
             passed_on(side).start()
+
+    tail = advance(1, first_step(0), tail, jnp.int32(2), True)
 
     for side in range(2):
 
@@ -427,46 +443,33 @@
             lax.fori_loop(0, 8, build, 0)
 
     def couple(slot, tail):
-        faces_of = [face(wsend[slot, side], side, 4 * (1 - side) * BLOCK) for side in range(2)]
-        result = jnp.concatenate([own_part[slot, 0], own_part[slot, 1]], axis=1)
-        for side in range(2):
-
-            @pl.when(has[side])
-            def _():
-                field_near(slot, 1 - side).wait_recv()
-
-            result = result + conduct(near[slot, side], (8 + 4 * side) * BLOCK, 4 * BLOCK)
-        result, tail = own_product(divided(result), tail, 2 * slot + 2)
+        ahead = [face(wsend[slot, side], side, 4 * (1 - side) * BLOCK) for side in range(2)]
+        result, tail = own_product(first_step(slot), tail, 2 * slot + 1)
         for side in range(2):
 
             @pl.when(has_far[side])
             def _():
                 field_far(slot, 1 - side).wait_recv()
 
-            ahead = faces_of[side] + face(far[slot, side], side, 4 * side * BLOCK)
+            ahead[side] = divide(
+                ahead[side] + face(far[slot, side], side, 4 * side * BLOCK),
+                face_recip[side, 0], face_recip[side, 1], face_recip[side, 2],
+            )
+        for side in range(2):
 
             @pl.when(has[side])
             def _():
                 part_near(slot, 1 - side).wait_recv()
 
-            ahead = divide(
-                ahead + part[slot, side],
-                face_recip[side, 0], face_recip[side, 1], face_recip[side, 2],
-            )
-            result = result + conduct(ahead, (8 + 4 * side) * BLOCK, 4 * BLOCK)
-        return advance(slot + 1, divided(result), tail)
-
-    lax.fori_loop(0, PAIRS, couple, tail)
-
-    result = jnp.concatenate([own_part[PAIRS, 0], own_part[PAIRS, 1]], axis=1)
-    for side in range(2):
-
-        @pl.when(has[side])
-        def _():
-            field_near(PAIRS, 1 - side).wait_recv()
-
-        result = result + conduct(near[PAIRS, side], (8 + 4 * side) * BLOCK, 4 * BLOCK)
-    value = divided(result)
+        result = result + received(ahead[0] + part[slot, 0], ahead[1] + part[slot, 1])
+        return divided(result), tail
+
+    def step(slot, tail):
+        value, tail = couple(slot, tail)
+        return advance(slot + 1, value, tail, 2 * slot + 2, True)
+
+    tail = lax.fori_loop(1, PAIRS, step, tail)
+    value, _ = couple(PAIRS, tail)
 
     places = []
     for block in range(8):
@@ -492,12 +495,12 @@
             passed_on(side).wait_send()
             for slot in range(PAIRS + 1):
                 field_near(slot, side).wait_send()
-            for slot in range(PAIRS):
+            for slot in range(1, PAIRS + 1):
                 part_near(slot, side).wait_send()
 
         @pl.when(has_far[side])
         def _():
-            for slot in range(PAIRS):
+            for slot in range(1, PAIRS + 1):
                 field_far(slot, side).wait_send()
 
     kept = jnp.where(first, early, late)
@@ -548,6 +551,7 @@
             pltpu.VMEM((PAIRS + 1, 2, STEPS, half), f32),
             pltpu.VMEM((PAIRS + 1, 2, STEPS, half), f32),
             pltpu.VMEM((PAIRS + 1, 2, STEPS, half), f32),
+            pltpu.VMEM((PAIRS + 1, STEPS, nodes), f32),
             pltpu.VMEM((PAIRS + 1, 2, STEPS, half), f32),
             pltpu.VMEM((PAIRS + 1, 2, STEPS, half), f32),
             pltpu.VMEM((STEPS, nodes), f32),

time: 45.3 us -> 41.7 us (0.921)
  Pallas kernels: 44.5 us -> 40.9 us
    pallas_call x1, Pallas kernels: 44.5 us -> 40.9 us  [per_device(): pl.pallas_call(kernel, out_shape=pltpu.VMEM(adj_source.shape, f32), in_sp...]
where the time goes in v3:
time: 41.7 us; the launch traced here: 41.6 us
  Pallas kernels  40.9 us (98%)
  local copies, waits for them, and re-layouts  0.63 us (2%)
    pallas_call x1, Pallas kernels, per_device(): pl.pallas_call(kernel, out_shape=pltpu.VMEM(adj_source.shape, f32), in_sp...  40.9 us

profile of v3, /device:TPU:257, one launch (start us, length us, event | category | flops | bytes accessed | tf_op | source)
XLA Modules:
  0.0 41.6 jit_solution(10397289227311786267)
XLA Ops:
  0.0 40.9 %window.1 = f32[16,2,512]{2,1,0:T(2,128)S(1)} custom-call(f32[16,2,512]{2,1,0:T(2,128)} %adj_hbm.1, f32[2,512]{1,0:T(2,128)} %term_hbm.1, f32[1,512]{1,0:T(1,128)} %bitcast.1, s32[8,7]{1,0:T(8,128)} %cols_hbm.1, s32[1,2,4]{2,1,0:T(2,128)} %faces_hbm.1, bf16[2,32,48]{2,1,0:T(8,128)(2,1)} %constant.6.clone.forward_hbm, ...), custom_call_target="tpu_custom_call" | custom-call | tf_op jit(solution)/shard_map/window/pallas_call | solution.py:520
  40.9 0.6 %copy.11 = f32[16,2,512]{2,1,0:T(2,128)} copy(f32[16,2,512]{2,1,0:T(2,128)S(1)} %window.1) | data formatting | bytes 131072

commit v4 on v3

--- a/solution.py
+++ b/solution.py
@@ -91,7 +91,7 @@
     blocks_hbm, out,
     adj, term, cap, cols, faces, forward, backward, coefs, blk,
     turned, names, mat_high, mat_low, face_high, face_low, diag, recip, face_recip, capacity,
-    meta, met, tiles, psend, precv, pown, wsend, near, far, own_part, part_send, part, total, ysend, yrecv,
+    meta, met, tiles, psend, precv, pown, wsend, near, far, own_part, part_send, part, middle, tails, total, ysend, yrecv,
     load_sems, first_send, first_recv, once_send, once_recv, last_sems, send_sems, recv_sems,
 ):
     group = lax.axis_index("tm")
@@ -99,10 +99,21 @@
     shards = lax.axis_size("space")
     other = 1 - group
     first = group == 0
-    has = (shard > 0, shard < shards - 1)
-    has_far = (shard > 1, shard < shards - 2)
-    beside = (jnp.maximum(shard - 1, 0), jnp.minimum(shard + 1, shards - 1))
-    beyond = (jnp.maximum(shard - 2, 0), jnp.minimum(shard + 2, shards - 1))
+    slow = jnp.where(lax.rem(shard, 4) >= 2, 1, 0)
+    fast = 1 - slow
+    order = (fast, slow)
+
+    def has(side):
+        return jnp.where(side == 0, shard > 0, shard < shards - 1)
+
+    def has_far(side):
+        return jnp.where(side == 0, shard > 1, shard < shards - 2)
+
+    def beside(side):
+        return jnp.clip(shard + 2 * side - 1, 0, shards - 1)
+
+    def beyond(side):
+        return jnp.clip(shard + 4 * side - 2, 0, shards - 1)
 
     barrier = pltpu.get_barrier_semaphore()
 
@@ -112,16 +123,16 @@
     greets = 1
     for side in range(2):
 
-        @pl.when(has_far[side])
-        def _():
-            greet((group, beyond[side]))
-
-        @pl.when(has[side])
-        def _():
-            greet((0, beside[side]))
-            greet((1, beside[side]))
-
-        greets = greets + 2 * has[side].astype(jnp.int32) + has_far[side].astype(jnp.int32)
+        @pl.when(has_far(side))
+        def _():
+            greet((group, beyond(side)))
+
+        @pl.when(has(side))
+        def _():
+            greet((0, beside(side)))
+            greet((1, beside(side)))
+
+        greets = greets + 2 * has(side).astype(jnp.int32) + has_far(side).astype(jnp.int32)
 
     greet((other, shard))
 
@@ -140,11 +151,11 @@
 
     for side in range(2):
 
-        @pl.when(jnp.logical_not(has_far[side]))
+        @pl.when(jnp.logical_not(has_far(side)))
         def _():
             far[:, side] = jnp.zeros_like(far[:, side])
 
-        @pl.when(jnp.logical_not(has[side]))
+        @pl.when(jnp.logical_not(has(side)))
         def _():
             near[:, side] = jnp.zeros_like(near[:, side])
             part[:, side] = jnp.zeros_like(part[:, side])
@@ -157,20 +168,23 @@
 
     ids = [faces[0, i // 4, i % 4] for i in range(8)]
     cap_row = cap[...]
-    capacity[...] = reorder(jnp.broadcast_to(cap_row, (8, 8 * BLOCK)), ids)
+    cap_own = reorder(jnp.broadcast_to(cap_row, (8, 8 * BLOCK)), ids)
     eye = lax.broadcasted_iota(jnp.int32, (BLOCK, BLOCK), 0) == lax.broadcasted_iota(
         jnp.int32, (BLOCK, BLOCK), 1
     )
     rows = [
         jnp.sum(jnp.where(eye, blk[ids[i], 0], 0.0), axis=0, keepdims=True) for i in range(8)
     ]
-    diag[...] = jnp.broadcast_to(jnp.concatenate(rows, axis=1), diag.shape)
-
-    def reciprocals(cap_own, diag_own):
-        imag = coefs[0:HALF, 1:2] * cap_own
+    diag_own = jnp.broadcast_to(jnp.concatenate(rows, axis=1), (8, 8 * BLOCK))
+    for half in range(2):
+        capacity[half] = cap_own[:, half * 4 * BLOCK : (half + 1) * 4 * BLOCK]
+        diag[half] = diag_own[:, half * 4 * BLOCK : (half + 1) * 4 * BLOCK]
+
+    def reciprocals(cap_part, diag_part):
+        imag = coefs[0:HALF, 1:2] * cap_part
         found = []
         for half in range(2):
-            real = coefs[half * HALF : (half + 1) * HALF, 0:1] * cap_own + diag_own
+            real = coefs[half * HALF : (half + 1) * HALF, 0:1] * cap_part + diag_part
             over = 1.0 / (real * real + imag * imag)
             found.append(real * over)
             if half == 0:
@@ -187,17 +201,20 @@
             axis=0,
         )
 
-    recip[0], recip[1], recip[2] = reciprocals(capacity[0:1, :], diag[0:1, :])
-
-    def divided(value):
-        return divide(value, recip[0], recip[1], recip[2])
+    for half in range(2):
+        recip[half, 0], recip[half, 1], recip[half, 2] = reciprocals(
+            capacity[half, 0:1], diag[half, 0:1]
+        )
+
+    def divided(value, half):
+        return divide(value, recip[half, 0], recip[half, 1], recip[half, 2])
 
     head_row = first & (lax.broadcasted_iota(jnp.int32, (HALF, 1), 0) == 0)
     for case in range(2):
         source = adj[:, case, :] + jnp.where(head_row, term[case : case + 1, :] * cap_row, 0.0)
-        field = divided(reorder(product(forward[group], source), ids))
-        psend[case, 0] = field[:, : 4 * BLOCK]
-        psend[case, 1] = field[:, 4 * BLOCK :]
+        spectrum = reorder(product(forward[group], source), ids)
+        psend[case, 0] = divided(spectrum[:, : 4 * BLOCK], 0)
+        psend[case, 1] = divided(spectrum[:, 4 * BLOCK :], 1)
 
     lower_half = lax.broadcasted_iota(jnp.int32, (1, LANES), 1) < BLOCK
     turned_eye = lax.broadcasted_iota(jnp.int32, (BLOCK, LANES), 0) == lax.rem(
@@ -219,15 +236,16 @@
     place_of = jnp.zeros_like(raw)
     for i in range(8):
         place_of = jnp.where(raw == ids[i], i, place_of)
-    place_of = jnp.where(raw >= 8, jnp.where(has[0], raw, -1), place_of)
-    place_of = jnp.where(raw >= 12, jnp.where(has[1], raw, -1), place_of)
+    place_of = jnp.where(raw >= 8, jnp.where(has(0), raw, -1), place_of)
+    place_of = jnp.where(raw >= 12, jnp.where(has(1), raw, -1), place_of)
     named = place_of.astype(jnp.float32)
     for side in range(2):
         meta[side, 0:16] = named[16 * side : 16 * side + 16]
         for row, table in ((16, capacity), (24, diag)):
             for pair in range(2):
-                lane = (2 * side + pair) * LANES
-                meta[side, row + 4 * pair : row + 4 * pair + 4] = table[0:4, lane : lane + LANES]
+                meta[side, row + 4 * pair : row + 4 * pair + 4] = table[
+                    side, 0:4, pair * LANES : (pair + 1) * LANES
+                ]
     for pair in range(4):
         wanted = [named[8 * pair + k : 8 * pair + k + 1] for k in range(7)]
 
@@ -238,8 +256,9 @@
                 tile = tile + jnp.where(wanted[k] == name, turned[pair, k], 0.0)
             high, low = split(tile)
             at = pl.ds(pl.multiple_of(place * BLOCK, BLOCK), BLOCK)
-            mat_high[at, pair * LANES : (pair + 1) * LANES] = high
-            mat_low[at, pair * LANES : (pair + 1) * LANES] = low
+            lanes = slice(pair % 2 * LANES, (pair % 2 + 1) * LANES)
+            mat_high[pair // 2, at, lanes] = high
+            mat_low[pair // 2, at, lanes] = low
             return carry
 
         lax.fori_loop(0, 16, build, 0)
@@ -256,7 +275,7 @@
         return remote(
             psend.at[case, side], precv.at[sender, 1 - side],
             first_send.at[2 * side + case], first_recv.at[2 * (1 - side) + sender],
-            (case, beside[side]),
+            (case, beside(side)),
         )
 
     first_own = remote(
@@ -266,13 +285,13 @@
     def matrix_rows(side):
         return remote(
             turned.at[2 * side + group, pl.ds(1, 6)], tiles.at[1 - side, group],
-            once_send.at[side], once_recv.at[1 - side], (group, beside[side]),
+            once_send.at[side], once_recv.at[1 - side], (group, beside(side)),
         )
 
     def row_facts(side):
         return remote(
             meta.at[side], met.at[1 - side],
-            once_send.at[2 + side], once_recv.at[3 - side], (group, beside[side]),
+            once_send.at[2 + side], once_recv.at[3 - side], (group, beside(side)),
         )
 
     def passed_on(side):
@@ -284,134 +303,150 @@
     def field_near(slot, side):
         return remote(
             wsend.at[slot, side], near.at[slot, 1 - side],
-            send_sems.at[slot, side], recv_sems.at[slot, 1 - side], (group, beside[side]),
+            send_sems.at[slot, 0, side], recv_sems.at[slot, 0, 1 - side], (group, beside(side)),
         )
 
     def field_far(slot, side):
         return remote(
             wsend.at[slot, side], far.at[slot, 1 - side],
-            send_sems.at[slot, 2 + side], recv_sems.at[slot, 3 - side], (group, beyond[side]),
+            send_sems.at[slot, 1, side], recv_sems.at[slot, 1, 1 - side], (group, beyond(side)),
         )
 
     def part_near(slot, side):
         return remote(
             part_send.at[slot, side], part.at[slot, 1 - side],
-            send_sems.at[slot, 4 + side], recv_sems.at[slot, 5 - side], (group, beside[side]),
-        )
-
-    for side in range(2):
-
-        @pl.when(has[side])
+            send_sems.at[slot, 2, side], recv_sems.at[slot, 2, 1 - side], (group, beside(side)),
+        )
+
+    for side in (slow, fast):
+
+        @pl.when(has(side))
         def _():
             for case in range(2):
                 first_halo(side, case, group).start()
 
     first_own.start()
 
-    def times(value, matrix_high, matrix_low):
+    def pieces_of(value):
         high, low = split(value)
-        both = jnp.dot(
-            jnp.concatenate([high, low], axis=0), matrix_high, preferred_element_type=jnp.float32
-        )
+        return high, jnp.concatenate([high, low], axis=0)
+
+    def times(pieces, matrix_high, matrix_low):
+        high, stacked = pieces
+        both = jnp.dot(stacked, matrix_high, preferred_element_type=jnp.float32)
         rest = jnp.dot(high, matrix_low, preferred_element_type=jnp.float32)
         return both[:STEPS] + both[STEPS:] + rest
 
-    def conduct(value, start, count):
-        return times(
-            value, mat_high[start : start + count, :], mat_low[start : start + count, :]
-        )
-
-    def received(from_lower, from_upper):
-        return conduct(jnp.concatenate([from_lower, from_upper], axis=1), 8 * BLOCK, 8 * BLOCK)
-
-    def face(value, side, start):
-        return times(
-            value, face_high[side, start : start + 4 * BLOCK], face_low[side, start : start + 4 * BLOCK]
-        )
+    def rows_of(side):
+        return pl.ds(pl.multiple_of(side * (4 * BLOCK), 4 * BLOCK), 4 * BLOCK)
+
+    def received(pieces, half, side):
+        rows = rows_of(2 + side)
+        return times(pieces, mat_high[half, rows, :], mat_low[half, rows, :])
+
+    def face(value, side, from_side):
+        rows = rows_of(from_side)
+        return times(pieces_of(value), face_high[side, rows, :], face_low[side, rows, :])
 
     real_rows = lax.broadcasted_iota(jnp.int32, (STEPS, 1), 0) <= HALF
     last = coefs[:, 2:3]
 
-    def own_product(value, tail, application):
-        total[...] += value
-        tail = tail + jnp.sum(value * last, axis=0, keepdims=True)
+    def note(value, half):
+        total[half] += value
+        weighted = value * last
+        tails[half] += weighted[0:8] + weighted[8:16] + weighted[16:24] + weighted[24:32]
+
+    def own_product(pieces, half, application):
         closes = lax.rem(application, SWEEPS) == SWEEPS - 1
-        fix = jnp.where(closes, tail, 0.0) * capacity[0:1, :]
-        tail = jnp.where(closes, 0.0, tail)
-        return conduct(value, 0, 8 * BLOCK) - jnp.where(real_rows, fix, 0.0), tail
-
-    def advance(slot, value, tail, application, paired):
-        wsend[slot, 0] = value[:, : 4 * BLOCK]
-        wsend[slot, 1] = value[:, 4 * BLOCK :]
-        for side in range(2):
-
-            @pl.when(has[side])
+        tail = jnp.sum(tails[half], axis=0, keepdims=True)
+        fix = jnp.where(closes, tail, 0.0) * capacity[half, 0:1]
+        tails[half] = jnp.where(closes, 0.0, tails[half])
+        result = times(
+            pieces, mat_high[half, 0 : 8 * BLOCK, :], mat_low[half, 0 : 8 * BLOCK, :]
+        )
+        return result - jnp.where(real_rows, fix, 0.0)
+
+    def send_field(slot, side, paired):
+        @pl.when(has(side))
+        def _():
+            field_near(slot, side).start()
+
+        if paired:
+
+            @pl.when(has_far(side))
             def _():
-                field_near(slot, side).start()
-
-        if paired:
-            for side in range(2):
-
-                @pl.when(has_far[side])
+                field_far(slot, side).start()
+
+    def advance(slot, slow_part, fast_part, pieces, application, paired):
+        for half, value in ((slow, slow_part), (fast, fast_part)):
+            value = divided(value + received(pieces, half, slow), half)
+            wsend[slot, half] = value
+            send_field(slot, half, paired)
+            note(value, half)
+        pieces = pieces_of(jnp.concatenate([wsend[slot, 0], wsend[slot, 1]], axis=1))
+        for half in (slow, fast):
+            result = own_product(pieces, half, application)
+            own_part[slot, half] = result
+            if paired:
+                part_send[slot, half] = divided(result, half)
+
+                @pl.when(has(half))
                 def _():
-                    field_far(slot, side).start()
-
-        result, tail = own_product(value, tail, application)
-        own_part[slot] = result
-        if paired:
-            result = divided(result)
-            part_send[slot, 0] = result[:, : 4 * BLOCK]
-            part_send[slot, 1] = result[:, 4 * BLOCK :]
-            for side in range(2):
-
-                @pl.when(has[side])
-                def _():
-                    part_near(slot, side).start()
-
-        return tail
-
-    def first_step(slot):
-        for side in range(2):
-
-            @pl.when(has[side])
-            def _():
-                field_near(slot, 1 - side).wait_recv()
-
-        return divided(own_part[slot] + received(near[slot, 0], near[slot, 1]))
-
+                    part_near(slot, half).start()
+
+    def near_of(slot, side):
+        @pl.when(has(side))
+        def _():
+            field_near(slot, 1 - side).wait_recv()
+
+        return pieces_of(near[slot, side])
+
+    def add_fast(slow_part, fast_part, pieces):
+        return slow_part + received(pieces, slow, fast), fast_part + received(pieces, fast, fast)
+
+    def begun(slot):
+        return add_fast(own_part[slot, slow], own_part[slot, fast], near_of(slot, fast))
+
+    total[...] = jnp.zeros_like(total)
+    tails[...] = jnp.zeros_like(tails)
     first_own.wait_recv()
-    value = jnp.concatenate([psend[group, 0] + pown[0], psend[group, 1] + pown[1]], axis=1)
-    total[...] = jnp.zeros_like(total)
-    result, tail = own_product(value, jnp.zeros((1, 8 * BLOCK), jnp.float32), jnp.int32(0))
+    halves = [psend[group, half] + pown[half] for half in range(2)]
+    for half in range(2):
+        note(halves[half], half)
+    pieces = pieces_of(jnp.concatenate(halves, axis=1))
+    slow_part = own_product(pieces, slow, jnp.int32(0))
+    fast_part = own_product(pieces, fast, jnp.int32(0))
     for side in range(2):
 
-        @pl.when(has[side])
+        @pl.when(has(side))
         def _():
             row_facts(side).start()
             matrix_rows(side).start()
 
-    for side in range(2):
-
-        @pl.when(has[side])
+    for side in order:
+
+        @pl.when(has(side))
         def _():
             for sender in range(2):
                 first_halo(1 - side, 0, sender).wait_recv()
 
-    result = result + received(precv[0, 0] + precv[1, 0], precv[0, 1] + precv[1, 1])
-    tail = advance(0, divided(result), tail, jnp.int32(1), False)
+        pieces = pieces_of(precv[0, side] + precv[1, side])
+        if side is fast:
+            slow_part, fast_part = add_fast(slow_part, fast_part, pieces)
+    advance(0, slow_part, fast_part, pieces, jnp.int32(1), False)
 
     for side in range(2):
 
-        @pl.when(has[side])
+        @pl.when(has(side))
         def _():
             matrix_rows(1 - side).wait_recv()
             passed_on(side).start()
 
-    tail = advance(1, first_step(0), tail, jnp.int32(2), True)
+    advance(1, *begun(0), near_of(0, slow), jnp.int32(2), True)
 
     for side in range(2):
 
-        @pl.when(has[side])
+        @pl.when(has(side))
         def _():
             row_facts(1 - side).wait_recv()
 
@@ -420,7 +455,7 @@
             jnp.concatenate([met[side, 24:25], met[side, 28:29]], axis=1),
         )
 
-        @pl.when(has[side])
+        @pl.when(has(side))
         def _():
             passed_on(side).wait_recv()
 
@@ -442,34 +477,45 @@
 
             lax.fori_loop(0, 8, build, 0)
 
-    def couple(slot, tail):
-        ahead = [face(wsend[slot, side], side, 4 * (1 - side) * BLOCK) for side in range(2)]
-        result, tail = own_product(first_step(slot), tail, 2 * slot + 1)
-        for side in range(2):
-
-            @pl.when(has_far[side])
-            def _():
-                field_far(slot, 1 - side).wait_recv()
-
-            ahead[side] = divide(
-                ahead[side] + face(far[slot, side], side, 4 * side * BLOCK),
-                face_recip[side, 0], face_recip[side, 1], face_recip[side, 2],
-            )
-        for side in range(2):
-
-            @pl.when(has[side])
-            def _():
-                part_near(slot, 1 - side).wait_recv()
-
-        result = result + received(ahead[0] + part[slot, 0], ahead[1] + part[slot, 1])
-        return divided(result), tail
-
-    def step(slot, tail):
-        value, tail = couple(slot, tail)
-        return advance(slot + 1, value, tail, 2 * slot + 2, True)
-
-    tail = lax.fori_loop(1, PAIRS, step, tail)
-    value, _ = couple(PAIRS, tail)
+    def ahead_of(slot, side, early):
+        @pl.when(has_far(side))
+        def _():
+            field_far(slot, 1 - side).wait_recv()
+
+        found = divide(
+            early + face(far[slot, side], side, side),
+            face_recip[side, 0], face_recip[side, 1], face_recip[side, 2],
+        )
+
+        @pl.when(has(side))
+        def _():
+            part_near(slot, 1 - side).wait_recv()
+
+        return pieces_of(found + part[slot, side])
+
+    def couple(slot):
+        early = [face(wsend[slot, side], side, 1 - side) for side in order]
+        slow_part, fast_part = begun(slot)
+        pieces = ahead_of(slot, fast, early[0])
+        slow_more, fast_more = received(pieces, slow, fast), received(pieces, fast, fast)
+        pieces = near_of(slot, slow)
+        for half, value in ((slow, slow_part), (fast, fast_part)):
+            value = divided(value + received(pieces, half, slow), half)
+            middle[half] = value
+            note(value, half)
+        pieces = pieces_of(jnp.concatenate([middle[0], middle[1]], axis=1))
+        slow_part = slow_more + own_product(pieces, slow, 2 * slot + 1)
+        fast_part = fast_more + own_product(pieces, fast, 2 * slot + 1)
+        return slow_part, fast_part, ahead_of(slot, slow, early[1])
+
+    def step(slot, carry):
+        advance(slot + 1, *couple(slot), 2 * slot + 2, True)
+        return carry
+
+    lax.fori_loop(1, PAIRS, step, 0)
+    slow_part, fast_part, pieces = couple(PAIRS)
+    for half, value in ((slow, slow_part), (fast, fast_part)):
+        total[half] += divided(value + received(pieces, half, slow), half)
 
     places = []
     for block in range(8):
@@ -477,7 +523,7 @@
         for i in range(1, 8):
             place = place + jnp.where(ids[i] == block, i, 0)
         places.append(place)
-    summed = product(backward[...], reorder(total[...] + value, places))
+    summed = product(backward[...], reorder(jnp.concatenate([total[0], total[1]], axis=1), places))
     early, late = summed[:HALF], summed[HALF:]
     ysend[...] = jnp.where(first, late, early)
     ycopy = remote(ysend, yrecv, last_sems.at[0], last_sems.at[1], (other, shard))
@@ -486,7 +532,7 @@
     first_own.wait_send()
     for side in range(2):
 
-        @pl.when(has[side])
+        @pl.when(has(side))
         def _():
             for case in range(2):
                 first_halo(side, case, group).wait_send()
@@ -498,7 +544,7 @@
             for slot in range(1, PAIRS + 1):
                 part_near(slot, side).wait_send()
 
-        @pl.when(has_far[side])
+        @pl.when(has_far(side))
         def _():
             for slot in range(1, PAIRS + 1):
                 field_far(slot, side).wait_send()
@@ -534,14 +580,14 @@
             pltpu.VMEM(blocks.shape, f32),
             pltpu.VMEM((4, 7, BLOCK, LANES), f32),
             pltpu.VMEM((32, LANES), i32),
-            pltpu.VMEM((16 * BLOCK, nodes), bf16),
-            pltpu.VMEM((16 * BLOCK, nodes), bf16),
+            pltpu.VMEM((2, 16 * BLOCK, half), bf16),
+            pltpu.VMEM((2, 16 * BLOCK, half), bf16),
             pltpu.VMEM((2, 8 * BLOCK, half), bf16),
             pltpu.VMEM((2, 8 * BLOCK, half), bf16),
-            pltpu.VMEM((8, nodes), f32),
-            pltpu.VMEM((3, HALF, nodes), f32),
+            pltpu.VMEM((2, 8, half), f32),
             pltpu.VMEM((2, 3, HALF, half), f32),
-            pltpu.VMEM((8, nodes), f32),
+            pltpu.VMEM((2, 3, HALF, half), f32),
+            pltpu.VMEM((2, 8, half), f32),
             pltpu.VMEM((2, 32, LANES), f32),
             pltpu.VMEM((2, 32, LANES), f32),
             pltpu.VMEM((2, 2, 6, BLOCK, LANES), f32),
@@ -551,10 +597,12 @@
             pltpu.VMEM((PAIRS + 1, 2, STEPS, half), f32),
             pltpu.VMEM((PAIRS + 1, 2, STEPS, half), f32),
             pltpu.VMEM((PAIRS + 1, 2, STEPS, half), f32),
-            pltpu.VMEM((PAIRS + 1, STEPS, nodes), f32),
             pltpu.VMEM((PAIRS + 1, 2, STEPS, half), f32),
             pltpu.VMEM((PAIRS + 1, 2, STEPS, half), f32),
-            pltpu.VMEM((STEPS, nodes), f32),
+            pltpu.VMEM((PAIRS + 1, 2, STEPS, half), f32),
+            pltpu.VMEM((2, STEPS, half), f32),
+            pltpu.VMEM((2, 8, half), f32),
+            pltpu.VMEM((2, STEPS, half), f32),
             pltpu.VMEM((HALF, nodes), f32),
             pltpu.VMEM((HALF, nodes), f32),
             dma((9,)),
@@ -563,8 +611,8 @@
             dma((6,)),
             dma((6,)),
             dma((2,)),
-            dma((PAIRS + 1, 6)),
-            dma((PAIRS + 1, 6)),
+            dma((PAIRS + 1, 3, 2)),
+            dma((PAIRS + 1, 3, 2)),
         ],
         compiler_params=pltpu.CompilerParams(
             collective_id=0, has_side_effects=True, vmem_limit_bytes=60 * 1024 * 1024

time: 41.7 us -> 40.7 us (0.976)
  Pallas kernels: 40.9 us -> 39.9 us
    pallas_call x1, Pallas kernels: 40.9 us -> 39.9 us  [per_device(): pl.pallas_call(kernel, out_shape=pltpu.VMEM(adj_source.shape, f32), in_sp...]
where the time goes in v4:
time: 40.7 us; the launch traced here: 40.5 us
  Pallas kernels  39.9 us (98%)
  local copies, waits for them, and re-layouts  0.63 us (2%)
    pallas_call x1, Pallas kernels, per_device(): pl.pallas_call(kernel, out_shape=pltpu.VMEM(adj_source.shape, f32), in_sp...  39.9 us

profile of v4, /device:TPU:257, one launch (start us, length us, event | category | flops | bytes accessed | tf_op | source)
XLA Modules:
  0.0 40.5 jit_solution(11246397683143327907)
XLA Ops:
  0.0 39.9 %window.1 = f32[16,2,512]{2,1,0:T(2,128)S(1)} custom-call(f32[16,2,512]{2,1,0:T(2,128)} %adj_hbm.1, f32[2,512]{1,0:T(2,128)} %term_hbm.1, f32[1,512]{1,0:T(1,128)} %bitcast.1, s32[8,7]{1,0:T(8,128)} %cols_hbm.1, s32[1,2,4]{2,1,0:T(2,128)} %faces_hbm.1, bf16[2,32,48]{2,1,0:T(8,128)(2,1)} %constant.6.clone.forward_hbm, ...), custom_call_target="tpu_custom_call" | custom-call | tf_op jit(solution)/shard_map/window/pallas_call | solution.py:566
  39.9 0.6 %copy.11 = f32[16,2,512]{2,1,0:T(2,128)} copy(f32[16,2,512]{2,1,0:T(2,128)S(1)} %window.1) | data formatting | bytes 131072

commit v5 on v4

--- a/solution.py
+++ b/solution.py
@@ -89,7 +89,7 @@
 def kernel(
     adj_hbm, term_hbm, cap_hbm, cols_hbm, faces_hbm, forward_hbm, backward_hbm, coefs_hbm,
     blocks_hbm, out,
-    adj, term, cap, cols, faces, forward, backward, coefs, blk,
+    adj, term, cap, cols, faces, forward, backward, coefs, own_blk, blk,
     turned, names, mat_high, mat_low, face_high, face_low, diag, recip, face_recip, capacity,
     meta, met, tiles, psend, precv, pown, wsend, near, far, own_part, part_send, part, middle, tails, total, ysend, yrecv,
     load_sems, first_send, first_recv, once_send, once_recv, last_sems, send_sems, recv_sems,
@@ -123,16 +123,12 @@
     greets = 1
     for side in range(2):
 
-        @pl.when(has_far(side))
-        def _():
-            greet((group, beyond(side)))
-
         @pl.when(has(side))
         def _():
             greet((0, beside(side)))
             greet((1, beside(side)))
 
-        greets = greets + 2 * has(side).astype(jnp.int32) + has_far(side).astype(jnp.int32)
+        greets = greets + 2 * has(side).astype(jnp.int32)
 
     greet((other, shard))
 
@@ -140,9 +136,10 @@
         pltpu.make_async_copy(source, target, load_sems.at[i])
         for i, (source, target) in enumerate(
             [
-                (faces_hbm, faces), (cols_hbm, cols), (adj_hbm, adj), (term_hbm, term),
-                (cap_hbm, cap), (coefs_hbm, coefs), (forward_hbm, forward),
-                (blocks_hbm, blk), (backward_hbm, backward),
+                (faces_hbm, faces), (blocks_hbm.at[:, 0], own_blk),
+                (coefs_hbm, coefs), (cap_hbm, cap), (adj_hbm, adj), (term_hbm, term),
+                (forward_hbm, forward), (cols_hbm, cols),
+                (blocks_hbm.at[:, pl.ds(1, 6)], blk), (backward_hbm, backward),
             ]
         )
     ]
@@ -163,7 +160,7 @@
             tiles[side] = jnp.zeros_like(tiles[side])
             met[side] = jnp.ones_like(met[side])
 
-    for load in loads:
+    for load in loads[:7]:
         load.wait()
 
     ids = [faces[0, i // 4, i % 4] for i in range(8)]
@@ -173,7 +170,7 @@
         jnp.int32, (BLOCK, BLOCK), 1
     )
     rows = [
-        jnp.sum(jnp.where(eye, blk[ids[i], 0], 0.0), axis=0, keepdims=True) for i in range(8)
+        jnp.sum(jnp.where(eye, own_blk[ids[i]], 0.0), axis=0, keepdims=True) for i in range(8)
     ]
     diag_own = jnp.broadcast_to(jnp.concatenate(rows, axis=1), (8, 8 * BLOCK))
     for half in range(2):
@@ -216,6 +213,72 @@
         psend[case, 0] = divided(spectrum[:, : 4 * BLOCK], 0)
         psend[case, 1] = divided(spectrum[:, 4 * BLOCK :], 1)
 
+    pl.semaphore_wait(barrier, greets)
+
+    def remote(source, target, send_sem, recv_sem, device):
+        return pltpu.make_async_remote_copy(
+            src_ref=source, dst_ref=target, send_sem=send_sem, recv_sem=recv_sem,
+            device_id=device, device_id_type=MESH,
+        )
+
+    def first_halo(side, case, sender):
+        return remote(
+            psend.at[case, side], precv.at[sender, 1 - side],
+            first_send.at[2 * side + case], first_recv.at[2 * (1 - side) + sender],
+            (case, beside(side)),
+        )
+
+    first_own = remote(
+        psend.at[other], pown, first_send.at[4], first_recv.at[4], (other, shard)
+    )
+
+    def matrix_rows(side):
+        return remote(
+            turned.at[2 * side + group, pl.ds(1, 6)], tiles.at[1 - side, group],
+            once_send.at[side], once_recv.at[1 - side], (group, beside(side)),
+        )
+
+    def row_facts(side):
+        return remote(
+            meta.at[side], met.at[1 - side],
+            once_send.at[2 + side], once_recv.at[3 - side], (group, beside(side)),
+        )
+
+    def passed_on(side):
+        return remote(
+            tiles.at[side, group], tiles.at[side, group],
+            once_send.at[4 + side], once_recv.at[4 + side], (other, shard),
+        )
+
+    def field_near(slot, side):
+        return remote(
+            wsend.at[slot, side], near.at[slot, 1 - side],
+            send_sems.at[slot, 0, side], recv_sems.at[slot, 0, 1 - side], (group, beside(side)),
+        )
+
+    def field_far(slot, side):
+        return remote(
+            wsend.at[slot, side], far.at[slot, 1 - side],
+            send_sems.at[slot, 1, side], recv_sems.at[slot, 1, 1 - side], (group, beyond(side)),
+        )
+
+    def part_near(slot, side):
+        return remote(
+            part_send.at[slot, side], part.at[slot, 1 - side],
+            send_sems.at[slot, 2, side], recv_sems.at[slot, 2, 1 - side], (group, beside(side)),
+        )
+
+    for side in (slow, fast):
+
+        @pl.when(has(side))
+        def _():
+            for case in range(2):
+                first_halo(side, case, group).start()
+
+    first_own.start()
+    for load in loads[7:]:
+        load.wait()
+
     lower_half = lax.broadcasted_iota(jnp.int32, (1, LANES), 1) < BLOCK
     turned_eye = lax.broadcasted_iota(jnp.int32, (BLOCK, LANES), 0) == lax.rem(
         lax.broadcasted_iota(jnp.int32, (BLOCK, LANES), 1), BLOCK
@@ -223,7 +286,8 @@
     for pair in range(4):
         left, right = ids[2 * pair], ids[2 * pair + 1]
         for k in range(7):
-            entry = jnp.concatenate([blk[left, k], blk[right, k]], axis=0)
+            both = [blk[at, k - 1] if k else own_blk[at] for at in (left, right)]
+            entry = jnp.concatenate(both, axis=0)
             entry = -entry.T
             if k == 0:
                 entry = jnp.where(turned_eye, 0.0, entry)
@@ -246,6 +310,13 @@
                 meta[side, row + 4 * pair : row + 4 * pair + 4] = table[
                     side, 0:4, pair * LANES : (pair + 1) * LANES
                 ]
+    for side in range(2):
+
+        @pl.when(has(side))
+        def _():
+            row_facts(side).start()
+            matrix_rows(side).start()
+
     for pair in range(4):
         wanted = [named[8 * pair + k : 8 * pair + k + 1] for k in range(7)]
 
@@ -262,70 +333,6 @@
             return carry
 
         lax.fori_loop(0, 16, build, 0)
-
-    pl.semaphore_wait(barrier, greets)
-
-    def remote(source, target, send_sem, recv_sem, device):
-        return pltpu.make_async_remote_copy(
-            src_ref=source, dst_ref=target, send_sem=send_sem, recv_sem=recv_sem,
-            device_id=device, device_id_type=MESH,
-        )
-
-    def first_halo(side, case, sender):
-        return remote(
-            psend.at[case, side], precv.at[sender, 1 - side],
-            first_send.at[2 * side + case], first_recv.at[2 * (1 - side) + sender],
-            (case, beside(side)),
-        )
-
-    first_own = remote(
-        psend.at[other], pown, first_send.at[4], first_recv.at[4], (other, shard)
-    )
-
-    def matrix_rows(side):
-        return remote(
-            turned.at[2 * side + group, pl.ds(1, 6)], tiles.at[1 - side, group],
-            once_send.at[side], once_recv.at[1 - side], (group, beside(side)),
-        )
-
-    def row_facts(side):
-        return remote(
-            meta.at[side], met.at[1 - side],
-            once_send.at[2 + side], once_recv.at[3 - side], (group, beside(side)),
-        )
-
-    def passed_on(side):
-        return remote(
-            tiles.at[side, group], tiles.at[side, group],
-            once_send.at[4 + side], once_recv.at[4 + side], (other, shard),
-        )
-
-    def field_near(slot, side):
-        return remote(
-            wsend.at[slot, side], near.at[slot, 1 - side],
-            send_sems.at[slot, 0, side], recv_sems.at[slot, 0, 1 - side], (group, beside(side)),
-        )
-
-    def field_far(slot, side):
-        return remote(
-            wsend.at[slot, side], far.at[slot, 1 - side],
-            send_sems.at[slot, 1, side], recv_sems.at[slot, 1, 1 - side], (group, beyond(side)),
-        )
-
-    def part_near(slot, side):
-        return remote(
-            part_send.at[slot, side], part.at[slot, 1 - side],
-            send_sems.at[slot, 2, side], recv_sems.at[slot, 2, 1 - side], (group, beside(side)),
-        )
-
-    for side in (slow, fast):
-
-        @pl.when(has(side))
-        def _():
-            for case in range(2):
-                first_halo(side, case, group).start()
-
-    first_own.start()
 
     def pieces_of(value):
         high, low = split(value)
@@ -416,13 +423,6 @@
     pieces = pieces_of(jnp.concatenate(halves, axis=1))
     slow_part = own_product(pieces, slow, jnp.int32(0))
     fast_part = own_product(pieces, fast, jnp.int32(0))
-    for side in range(2):
-
-        @pl.when(has(side))
-        def _():
-            row_facts(side).start()
-            matrix_rows(side).start()
-
     for side in order:
 
         @pl.when(has(side))
@@ -435,14 +435,14 @@
             slow_part, fast_part = add_fast(slow_part, fast_part, pieces)
     advance(0, slow_part, fast_part, pieces, jnp.int32(1), False)
 
+    advance(1, *begun(0), near_of(0, slow), jnp.int32(2), True)
+
     for side in range(2):
 
         @pl.when(has(side))
         def _():
             matrix_rows(1 - side).wait_recv()
             passed_on(side).start()
-
-    advance(1, *begun(0), near_of(0, slow), jnp.int32(2), True)
 
     for side in range(2):
 
@@ -577,7 +577,8 @@
             pltpu.VMEM(forward.shape, bf16),
             pltpu.VMEM(backward.shape, bf16),
             pltpu.VMEM(coefs.shape, f32),
-            pltpu.VMEM(blocks.shape, f32),
+            pltpu.VMEM((8, BLOCK, BLOCK), f32),
+            pltpu.VMEM((8, 6, BLOCK, BLOCK), f32),
             pltpu.VMEM((4, 7, BLOCK, LANES), f32),
             pltpu.VMEM((32, LANES), i32),
             pltpu.VMEM((2, 16 * BLOCK, half), bf16),
@@ -605,7 +606,7 @@
             pltpu.VMEM((2, STEPS, half), f32),
             pltpu.VMEM((HALF, nodes), f32),
             pltpu.VMEM((HALF, nodes), f32),
-            dma((9,)),
+            dma((10,)),
             dma((5,)),
             dma((5,)),
             dma((6,)),

time: 40.7 us -> 40.5 us (level)
  no operation moved by 1% of the time
where the time goes in v5:
time: 40.5 us; the launch traced here: 40.3 us
  Pallas kernels  39.7 us (98%)
  local copies, waits for them, and re-layouts  0.63 us (2%)
    pallas_call x1, Pallas kernels, per_device(): pl.pallas_call(kernel, out_shape=pltpu.VMEM(adj_source.shape, f32), in_sp...  39.7 us

profile of v5, /device:TPU:257, one launch (start us, length us, event | category | flops | bytes accessed | tf_op | source)
XLA Modules:
  0.0 40.3 jit_solution(17281725879619837969)
XLA Ops:
  0.0 39.7 %window.1 = f32[16,2,512]{2,1,0:T(2,128)S(1)} custom-call(f32[16,2,512]{2,1,0:T(2,128)} %adj_hbm.1, f32[2,512]{1,0:T(2,128)} %term_hbm.1, f32[1,512]{1,0:T(1,128)} %bitcast.1, s32[8,7]{1,0:T(8,128)} %cols_hbm.1, s32[1,2,4]{2,1,0:T(2,128)} %faces_hbm.1, bf16[2,32,48]{2,1,0:T(8,128)(2,1)} %constant.6.clone.forward_hbm, ...), custom_call_target="tpu_custom_call" | custom-call | tf_op jit(solution)/shard_map/window/pallas_call | solution.py:566
  39.7 0.6 %copy.11 = f32[16,2,512]{2,1,0:T(2,128)} copy(f32[16,2,512]{2,1,0:T(2,128)S(1)} %window.1) | data formatting | bytes 131072

commit v6 on v5

--- a/solution.py
+++ b/solution.py
@@ -373,8 +373,10 @@
         )
         return result - jnp.where(real_rows, fix, 0.0)
 
+    far_waits = (lax.rem(shard, 4) == 1) | (lax.rem(shard, 4) == 2)
+
     def send_field(slot, side, paired):
-        @pl.when(has(side))
+        @pl.when(has(side) & jnp.logical_not(far_waits))
         def _():
             field_near(slot, side).start()
 
@@ -383,12 +385,17 @@
             @pl.when(has_far(side))
             def _():
                 field_far(slot, side).start()
+
+        @pl.when(has(side) & far_waits)
+        def _():
+            field_near(slot, side).start()
 
     def advance(slot, slow_part, fast_part, pieces, application, paired):
         for half, value in ((slow, slow_part), (fast, fast_part)):
             value = divided(value + received(pieces, half, slow), half)
             wsend[slot, half] = value
-            send_field(slot, half, paired)
+            if half is slow:
+                send_field(slot, half, paired)
             note(value, half)
         pieces = pieces_of(jnp.concatenate([wsend[slot, 0], wsend[slot, 1]], axis=1))
         for half in (slow, fast):
@@ -400,6 +407,9 @@
                 @pl.when(has(half))
                 def _():
                     part_near(slot, half).start()
+
+            if half is slow:
+                send_field(slot, fast, paired)
 
     def near_of(slot, side):
         @pl.when(has(side))

time: 40.5 us -> 40.4 us (level)
  no operation moved by 1% of the time
where the time goes in v6:
time: 40.4 us; the launch traced here: 40.3 us
  Pallas kernels  39.6 us (98%)
  local copies, waits for them, and re-layouts  0.63 us (2%)
    pallas_call x1, Pallas kernels, per_device(): pl.pallas_call(kernel, out_shape=pltpu.VMEM(adj_source.shape, f32), in_sp...  39.6 us

profile of v6, /device:TPU:257, one launch (start us, length us, event | category | flops | bytes accessed | tf_op | source)
XLA Modules:
  0.0 40.3 jit_solution(18278012877350156162)
XLA Ops:
  0.0 39.6 %window.1 = f32[16,2,512]{2,1,0:T(2,128)S(1)} custom-call(f32[16,2,512]{2,1,0:T(2,128)} %adj_hbm.1, f32[2,512]{1,0:T(2,128)} %term_hbm.1, f32[1,512]{1,0:T(1,128)} %bitcast.1, s32[8,7]{1,0:T(8,128)} %cols_hbm.1, s32[1,2,4]{2,1,0:T(2,128)} %faces_hbm.1, bf16[2,32,48]{2,1,0:T(8,128)(2,1)} %constant.6.clone.forward_hbm, ...), custom_call_target="tpu_custom_call" | custom-call | tf_op jit(solution)/shard_map/window/pallas_call | solution.py:576
  39.6 0.6 %copy.11 = f32[16,2,512]{2,1,0:T(2,128)} copy(f32[16,2,512]{2,1,0:T(2,128)S(1)} %window.1) | data formatting | bytes 131072
